TPU v7x, 32 devices: a whole 2x2x4 slice. The times are simulated.
32 devices in a mesh: facet: 8 (over y, x, core), chan: 4 (over z).
Axes of the slice: x: 2, y: 2, z: 4, core: 2. Of those that a mesh axis runs over, the one named last changes fastest.
Arguments:
- visibilities: float32 [8, 4, 4, 2, 256], P('facet', 'chan'), may hold values from -6 to 6
- positions: float32 [8, 4, 4, 2, 256], P('facet', 'chan'), may hold values from 4 to 251
- tracks: int32 [8, 4, 4, 4], P('facet', 'chan'), may hold values from 0 to 1
- counts: int32 [8, 4, 4], P('facet', 'chan'), may hold values from 0 to 4, as said below
- screens: float32 [8, 4, 2, 256, 256], P('facet', 'chan'), may hold values from 0.25 to 4
- offsets: int32 [8, 4, 2, 2], P('facet', 'chan'), may hold values from 0 to 4095, as said below
Outputs:
- image: float32 [2048, 16384], P('facet', 'chan')
Inputs may be any that keep to these rules, and one draw needn't show every extreme that they name: Of the 4 block slots from source c to owner d, the first counts[f, d, c] carry data; in every draw some owner receives 4 blocks from every source. Row offsets are below 256 and column offsets below 4096.
All inputs are finite; a program needn't handle non-finite values.
Results may differ from a plain program's by a relative error of at most 0.0003.
Values sent between devices are 32-bit elements; how exact they have to be, the bound alone decides.
No kernel may reach another device: no remote copies, remote signals or barrier semaphores. Data moves between devices by JAX's collectives and lax.ppermute only.
A program may use at most 64 MiB of HBM per device.

v0:
```python
import math

import jax
import jax.numpy as jnp
from jax import lax
from jax.sharding import PartitionSpec as P

TAPS = 8
STRIP = 256
BAND = 4096


def from_behind(value, axis, steps):
    count = lax.axis_size(axis)
    pairs = [(source, (source + steps) % count) for source in range(count)]
    return lax.ppermute(value, axis, pairs)


def taper_weight(offset):
    return jnp.where(jnp.abs(offset) < TAPS / 2, jnp.cos(jnp.pi * offset / TAPS) ** 2, 0.0)


def grid_blocks(got_vis, got_pos, own_tracks, own_counts, subgrids, grid_side):
    sources = got_vis.shape[0]
    slot_rows = got_vis.shape[2]
    capacity = own_tracks.shape[1]
    per_block = slot_rows // capacity
    block_index = jnp.arange(slot_rows, dtype=jnp.int32) // per_block
    live_mask = (block_index[None, :] < own_counts[:, None]).astype(jnp.float32)
    choose = (block_index[None, :] == jnp.arange(capacity, dtype=jnp.int32)[:, None]).astype(
        jnp.int32
    )
    target = jnp.sum(own_tracks[:, :, None] * choose[None, :, :], axis=1)
    all_rows = sources * slot_rows
    block_rows = 512
    block_turns = all_rows // block_rows
    u_position = got_pos[:, 0].reshape(block_turns, block_rows)
    v_position = got_pos[:, 1].reshape(block_turns, block_rows)
    real_part = (got_vis[:, 0] * live_mask).reshape(block_turns, block_rows)
    imag_part = (got_vis[:, 1] * live_mask).reshape(block_turns, block_rows)
    targets = target.reshape(block_turns, block_rows)
    cell_ids = jnp.arange(grid_side, dtype=jnp.float32)
    subgrid_ids = jnp.arange(subgrids, dtype=jnp.int32)

    def accumulate(grid_sum, pieces):
        u_rows, v_rows, real_rows, imag_rows, target_rows = pieces
        row_kernel = taper_weight(cell_ids[None, :] - u_rows[:, None])
        col_kernel = taper_weight(cell_ids[None, :] - v_rows[:, None])
        right_side = jnp.concatenate(
            [real_rows[:, None] * col_kernel, imag_rows[:, None] * col_kernel], axis=1
        )
        select = (target_rows[:, None] == subgrid_ids[None, :]).astype(jnp.float32)
        left_side = (row_kernel[:, None, :] * select[:, :, None]).reshape(
            block_rows, subgrids * grid_side
        )
        product = lax.dot_general(
            left_side,
            right_side,
            (((0,), (0,)), ((), ())),
            precision=lax.Precision.HIGHEST,
            preferred_element_type=jnp.float32,
        )
        return (grid_sum + product, None)

    start_grid = jnp.zeros((subgrids * grid_side, 2 * grid_side), jnp.float32)
    grids, _ = lax.scan(
        accumulate, start_grid, (u_position, v_position, real_part, imag_part, targets)
    )
    return grids


def screened_images(grids, screen_set, norm_scale):
    subgrids = screen_set.shape[0]
    grid_side = screen_set.shape[-1]
    cells = jnp.arange(grid_side, dtype=jnp.int32)
    turn = cells[:, None] * cells[None, :] % grid_side
    angle = turn.astype(jnp.float32) * (2.0 * math.pi / grid_side)
    cos_table = jnp.cos(angle)
    sin_table = jnp.sin(angle)
    results = []
    for sub_index in range(subgrids):
        grid_real = grids[sub_index * grid_side : (sub_index + 1) * grid_side, :grid_side]
        grid_imag = grids[sub_index * grid_side : (sub_index + 1) * grid_side, grid_side:]
        upper_sum = jnp.dot(
            cos_table,
            grid_real,
            precision=lax.Precision.HIGHEST,
            preferred_element_type=jnp.float32,
        ) + jnp.dot(
            sin_table,
            grid_imag,
            precision=lax.Precision.HIGHEST,
            preferred_element_type=jnp.float32,
        )
        lower_sum = jnp.dot(
            cos_table,
            grid_imag,
            precision=lax.Precision.HIGHEST,
            preferred_element_type=jnp.float32,
        ) - jnp.dot(
            sin_table,
            grid_real,
            precision=lax.Precision.HIGHEST,
            preferred_element_type=jnp.float32,
        )
        real_image = lax.dot_general(
            upper_sum,
            cos_table,
            (((1,), (1,)), ((), ())),
            precision=lax.Precision.HIGHEST,
            preferred_element_type=jnp.float32,
        )
        real_image = real_image + lax.dot_general(
            lower_sum,
            sin_table,
            (((1,), (1,)), ((), ())),
            precision=lax.Precision.HIGHEST,
            preferred_element_type=jnp.float32,
        )
        results.append(screen_set[sub_index] * real_image * norm_scale)
    return results


def shards(visibilities, positions, tracks, counts, screens, offsets):
    got_vis, got_pos = (
        lax.all_to_all(visibilities[0, 0], "chan", split_axis=0, concat_axis=0, tiled=True),
        lax.all_to_all(positions[0, 0], "chan", split_axis=0, concat_axis=0, tiled=True),
    )
    screen_set = screens[0, 0]
    corners = offsets[0, 0]
    grid_side = screen_set.shape[-1]
    grids = grid_blocks(
        got_vis, got_pos, tracks[0, 0], counts[0, 0], screen_set.shape[0], grid_side
    )
    owner_rows = got_vis.shape[0] * got_vis.shape[2]
    norm_scale = 1.0 / (2.0 * math.sqrt(owner_rows))
    pictures = screened_images(grids, screen_set, norm_scale)
    canvas = jnp.zeros((STRIP + grid_side, BAND + grid_side), jnp.float32)
    for sub_index in range(len(pictures)):
        row_start = corners[sub_index, 0]
        col_start = corners[sub_index, 1]
        current = lax.dynamic_slice(canvas, (row_start, col_start), (grid_side, grid_side))
        canvas = lax.dynamic_update_slice(
            canvas, current + pictures[sub_index], (row_start, col_start)
        )
    arrived_rows = from_behind(canvas[STRIP:], "facet", 1)
    folded = canvas[:STRIP].at[:grid_side].add(arrived_rows)
    arrived_cols = from_behind(folded[:, BAND:], "chan", 1)
    return folded[:, :BAND].at[:, :grid_side].add(arrived_cols)


def solution(mesh):
    return jax.shard_map(
        shards,
        mesh=mesh,
        in_specs=(
            P("facet", "chan", None, None, None),
            P("facet", "chan", None, None, None),
            P("facet", "chan", None, None),
            P("facet", "chan", None),
            P("facet", "chan", None, None, None),
            P("facet", "chan", None, None),
        ),
        out_specs=P("facet", "chan"),
        check_vma=False,
    )
```

profile of v0, /device:TPU:0, one launch (start us, length us, event | category | flops | bytes accessed | tf_op | source)
XLA Modules:
  0.0 136.7 jit_solution(14648077859532913197)
XLA Ops:
  0.0 6.3 %all-to-all-start.1 = ((f32[4,2,256]{2,1,0:T(2,128)}), f32[4,2,256]{2,1,0:T(2,128)S(1)}, u32[]{:S(2)}, u32[]{:S(2)}) async-start(f32[4,2,256]{2,1,0:T(2,128)} %bitcast.54), calls=%async_computation.1 | async-start | bytes 16384 | tf_op jit(solution)/shard_map/all_to_all | solution.py:126
  9.1 1.5 %fusion.111 = (s32[1,1]{1,0:T(1,128)}, s32[1,1]{1,0:T(1,128)}, s32[1,1]{1,0:T(1,128)}, s32[1,1]{1,0:T(1,128)}) fusion(s32[2,2]{1,0:T(2,128)} %bitcast.57), kind=kLoop, calls=%fused_computation.134 | loop fusion | bytes 32 | tf_op jit(solution)/shard_map/slice | solution.py:141
  18.2 5.1 %all-to-all-start = ((f32[4,2,256]{2,1,0:T(2,128)}), f32[4,2,256]{2,1,0:T(2,128)S(1)}, u32[]{:S(2)}, u32[]{:S(2)}) async-start(f32[4,2,256]{2,1,0:T(2,128)} %bitcast.55), calls=%async_computation | async-start | bytes 16384 | tf_op jit(solution)/shard_map/all_to_all | solution.py:127
  23.4 5.5 %all-to-all-done = f32[4,2,256]{2,1,0:T(2,128)S(1)} async-done(((f32[4,2,256]{2,1,0:T(2,128)}), f32[4,2,256]{2,1,0:T(2,128)S(1)}, u32[]{:S(2)}, u32[]{:S(2)}) %all-to-all-start) | async-done | bytes 8224 | tf_op jit(solution)/shard_map/all_to_all | solution.py:127
  29.0 14.1 %while.18 = (s32[]{:T(128)}, f32[512,512]{1,0:T(8,128)S(1)}, f32[2,512]{1,0:T(2,128)S(1)}, s32[2,512]{1,0:T(2,128)S(1)}, f32[2,512]{1,0:T(2,128)S(1)}, /*index=5...) while((s32[]{:T(128)}, f32[512,512]{1,0:T(8,128)S(1)}, ...), condition=%wide.region_2.3_spmd.clone.clone, body=%wide.region_1.2_spmd.clone.clone.sunk | while | flops 1613498368 | bytes 9484411 | solution.py:66
  29.2 1.9 %fusion.123 = f32[512,256]{1,0:T(8,128)S(1)} fusion(f32[512]{0:T(512)S(1)} %bitcast.51), kind=kLoop, calls=%fused_computation.21.clone.1 | loop fusion | flops 786432 | bytes 526336 | tf_op jit(solution)/shard_map/while/body/eval_jaxpr/jit(_where)/select_n | solution.py:20
  31.9 1.9 %fusion.124 = (f32[512,256]{1,0:T(8,128)S(1)}, f32[512,256]{1,0:T(8,128)S(1)}) fusion(f32[512]{0:T(512)S(1)} %bitcast.49, f32[512]{0:T(512)S(1)} %bitcast.50, f32[512]{0:T(512)S(1)} %bitcast.48), kind=kLoop, calls=%fused_computation.17.clone.1 | loop fusion | flops 1048576 | bytes 1054720 | tf_op jit(solution)/shard_map/while/body/eval_jaxpr/mul | solution.py:50
  33.8 2.1 %convolution_add_fusion.6 = f32[512,512]{1,0:T(8,128)S(1)} fusion(f32[512,512]{1,0:T(8,128)S(1)} %bitcast.46, f32[512,256]{1,0:T(8,128)S(1)} %get-tuple-element.311, f32[512,256]{1,0:T(8,128)S(1)} %get-tuple-element.312, f32[512,512]{1,0:T(8,128)S(1)} %get-tuple-element.323, pred[]{:T(512)S(6)} %compare.25), kind=kOutput, calls=%fused_computation.2.clone.1 | convolution fusion | flops 1611399168 | bytes 4194305 | tf_op jit(solution)/shard_map/while/body/eval_jaxpr/dot_general | solution.py:56
  36.2 1.9 %fusion.123 = f32[512,256]{1,0:T(8,128)S(1)} fusion(f32[512]{0:T(512)S(1)} %bitcast.51), kind=kLoop, calls=%fused_computation.21.clone.1 | loop fusion | flops 786432 | bytes 526336 | tf_op jit(solution)/shard_map/while/body/eval_jaxpr/jit(_where)/select_n | solution.py:20
  38.8 1.9 %fusion.124 = (f32[512,256]{1,0:T(8,128)S(1)}, f32[512,256]{1,0:T(8,128)S(1)}) fusion(f32[512]{0:T(512)S(1)} %bitcast.49, f32[512]{0:T(512)S(1)} %bitcast.50, f32[512]{0:T(512)S(1)} %bitcast.48), kind=kLoop, calls=%fused_computation.17.clone.1 | loop fusion | flops 1048576 | bytes 1054720 | tf_op jit(solution)/shard_map/while/body/eval_jaxpr/mul | solution.py:50
  40.8 2.1 %convolution_add_fusion.6 = f32[512,512]{1,0:T(8,128)S(1)} fusion(f32[512,512]{1,0:T(8,128)S(1)} %bitcast.46, f32[512,256]{1,0:T(8,128)S(1)} %get-tuple-element.311, f32[512,256]{1,0:T(8,128)S(1)} %get-tuple-element.312, f32[512,512]{1,0:T(8,128)S(1)} %get-tuple-element.323, pred[]{:T(512)S(6)} %compare.25), kind=kOutput, calls=%fused_computation.2.clone.1 | convolution fusion | flops 1611399168 | bytes 4194305 | tf_op jit(solution)/shard_map/while/body/eval_jaxpr/dot_general | solution.py:56
  49.9 1.4 convolution_subtract_fusion
  51.3 1.4 %convolution_add_fusion.4 = f32[256,256]{1,0:T(8,128)S(1)} fusion(f32[256,256]{1,0:T(8,128)S(1)} %fusion.44, f32[512,512]{1,0:T(8,128)S(1)} %get-tuple-element.177), kind=kOutput, calls=%fused_computation.38 | convolution fusion | flops 202309632 | bytes 786432 | tf_op jit(solution)/shard_map/dot_general | solution.py:89
  54.1 1.6 %convolution_add_fusion.2 = f32[256,256]{1,0:T(8,128)S(1)} fusion(f32[256,256]{1,0:T(8,128)S(1)} %fusion.38, f32[512,512]{1,0:T(8,128)S(1)} %get-tuple-element.177), kind=kOutput, calls=%fused_computation.34 | convolution fusion | flops 202309632 | bytes 786432 | tf_op jit(solution)/shard_map/dot_general | solution.py:89
  57.0 1.4 %fusion.24 = f32[256,256]{1,0:T(8,128)S(1)} fusion(f32[256,256]{1,0:T(8,128)S(1)} %fusion.53, f32[256,256]{1,0:T(8,128)S(1)} %convolution_subtract_fusion.1, f32[1,1,2,256,256]{4,3,2,1,0:T(8,128)S(1)} %copy-done.1), kind=kOutput, calls=%fused_computation.39 | convolution fusion | flops 202440704 | bytes 1048576 | tf_op jit(solution)/shard_map/dot_general | solution.py:113
  58.4 4.0 %broadcast_in_dim.12 = f32[512,4352]{1,0:T(8,128)} broadcast(f32[]{:T(128)} %constant.147.clone.1), dimensions={} | broadcast | bytes 8912900 | tf_op jit(solution)/shard_map/broadcast_in_dim | solution.py:138
  62.4 3.5 %dynamic_update_slice.6 = f32[512,4352]{1,0:T(8,128)} dynamic-update-slice(f32[512,4352]{1,0:T(8,128)} %broadcast_in_dim.12, f32[256,256]{1,0:T(8,128)S(1)} %fusion.24, s32[]{:T(128)S(6)} %select_n.75, s32[]{:T(128)S(6)} %select_n.76) | dynamic-update-slice | bytes 524292 | tf_op jit(solution)/shard_map/dynamic_update_slice | solution.py:143
  65.9 2.4 %fusion.26 = f32[256,256]{1,0:T(8,128)S(1)} fusion(f32[256,256]{1,0:T(8,128)S(1)} %fusion.49, f32[256,256]{1,0:T(8,128)S(1)} %convolution_subtract_fusion, f32[1,1,2,256,256]{4,3,2,1,0:T(8,128)S(1)} %copy-done.1, f32[512,4352]{1,0:T(8,128)} %dynamic_update_slice.6, s32[]{:T(128)S(6)} %select_n.77, s32[]{:T(128)S(6)} %select_n.78), kind=kOutput, calls=%fused_computation.41 | convolution fusion | flops 202506240 | bytes 1310728 | tf_op jit(solution)/shard_map/dot_general | solution.py:113
  68.2 3.6 %dynamic_update_slice.7 = f32[512,4352]{1,0:T(8,128)} dynamic-update-slice(f32[512,4352]{1,0:T(8,128)} %dynamic_update_slice.6, f32[256,256]{1,0:T(8,128)S(1)} %fusion.26, s32[]{:T(128)S(6)} %select_n.77, s32[]{:T(128)S(6)} %select_n.78) | dynamic-update-slice | bytes 524292 | tf_op jit(solution)/shard_map/dynamic_update_slice | solution.py:143
  71.8 2.7 %slice.114 = f32[256,4352]{1,0:T(8,128)S(1)} slice(f32[512,4352]{1,0:T(8,128)} %dynamic_update_slice.7), slice={[256:512], [0:4352]} | slice | bytes 8912896 | tf_op jit(solution)/shard_map/slice | solution.py:146
  74.6 51.6 %collective-permute-done = f32[256,4352]{1,0:T(8,128)S(1)} collective-permute-done((f32[256,4352]{1,0:T(8,128)S(1)}, f32[256,4352]{1,0:T(8,128)S(1)}, u32[]{:S(2)}, u32[]{:S(2)}) %collective-permute-start) | collective-permute-done | bytes 4456480 | tf_op jit(solution)/shard_map/ppermute | solution.py:16
  128.5 2.5 %slice.115 = f32[256,4096]{1,0:T(8,128)} slice(f32[256,4352]{1,0:T(8,128)S(1)} %slice_add_fusion), slice={[0:256], [0:4096]} | slice | bytes 8388608 | tf_op jit(solution)/shard_map/slice | solution.py:149
  131.0 4.3 %collective-permute-done.1 = f32[256,256]{1,0:T(8,128)S(1)} collective-permute-done((f32[256,256]{1,0:T(8,128)S(1)}, f32[256,256]{1,0:T(8,128)S(1)}, u32[]{:S(2)}, u32[]{:S(2)}) %collective-permute-start.1) | collective-permute-done | bytes 262176 | tf_op jit(solution)/shard_map/ppermute | solution.py:16
  135.3 1.4 %fusion.30 = f32[256,4096]{1,0:T(8,128)} fusion(f32[256,4096]{1,0:T(8,128)} %slice.115, f32[256,256]{1,0:T(8,128)S(1)} %collective-permute-done.1, f32[256,4352]{1,0:T(8,128)S(1)} %slice_add_fusion, pred[]{:T(512)} %compare_reduce_fusion), kind=kLoop, calls=%fused_computation.49 | loop fusion | flops 131072 | bytes 786944 | tf_op jit(solution)/shard_map/scatter-add | solution.py:149
  (50 shorter events, 16.7 us)
Async XLA Ops:
  0.0 18.2 %all-to-all-start.1 = ((f32[4,2,256]{2,1,0:T(2,128)}), f32[4,2,256]{2,1,0:T(2,128)S(1)}, u32[]{:S(2)}, u32[]{:S(2)}) async-start(f32[4,2,256]{2,1,0:T(2,128)} %bitcast.54), calls=%async_computation.1 | async-start | bytes 16384 | tf_op jit(solution)/shard_map/all_to_all | solution.py:126
  18.2 10.7 %all-to-all-start = ((f32[4,2,256]{2,1,0:T(2,128)}), f32[4,2,256]{2,1,0:T(2,128)S(1)}, u32[]{:S(2)}, u32[]{:S(2)}) async-start(f32[4,2,256]{2,1,0:T(2,128)} %bitcast.55), calls=%async_computation | async-start | bytes 16384 | tf_op jit(solution)/shard_map/all_to_all | solution.py:127
  47.2 9.8 %copy-start.1 = (f32[1,1,2,256,256]{4,3,2,1,0:T(8,128)S(1)}, f32[1,1,2,256,256]{4,3,2,1,0:T(8,128)}, u32[]{:S(2)}) copy-start(f32[1,1,2,256,256]{4,3,2,1,0:T(8,128)} %param.18) | copy-start | bytes 1572868
  71.8 54.4 %copy-start = (f32[512,4352]{1,0:T(8,128)S(1)}, f32[512,4352]{1,0:T(8,128)}, u32[]{:S(2)}) copy-start(f32[512,4352]{1,0:T(8,128)} %dynamic_update_slice.7) | copy-start | bytes 26738692
  74.5 51.7 %collective-permute-start = (f32[256,4352]{1,0:T(8,128)S(1)}, f32[256,4352]{1,0:T(8,128)S(1)}, u32[]{:S(2)}, u32[]{:S(2)}) collective-permute-start(f32[256,4352]{1,0:T(8,128)S(1)} %slice.114), channel_id=1, source_target_pairs={{0,4},{4,8},{8,12},{12,16},{16,20},{20,24},{24,28},{28,0},{1,5},{5... | collective-permute-start | bytes 13369352 | tf_op jit(solution)/shard_map/ppermute | solution.py:16
  126.7 8.6 %collective-permute-start.1 = (f32[256,256]{1,0:T(8,128)S(1)}, f32[256,256]{1,0:T(8,128)S(1)}, u32[]{:S(2)}, u32[]{:S(2)}) collective-permute-start(f32[256,256]{1,0:T(8,128)S(1)} %slice.117), channel_id=1, source_target_pairs={{0,1},{1,2},{2,3},{3,0},{4,5},{5,6},{6,7},{7,4},{8,9},{9,10},{10,1... | collective-permute-start | bytes 786440 | tf_op jit(solution)/shard_map/ppermute | solution.py:16
where the time goes:
time: 138 us; the launch traced here: 137 us
  waiting for transfers between devices  61.4 us (44%)
  matrix products  21.8 us (16%)
  local copies, waits for them, and re-layouts  19.1 us (14%)
  other arithmetic  13.7 us (10%)
  starting transfers between devices  12.6 us (9%)
  between operations  7.75 us (6%)
    ppermute x2, waiting for transfers between devices, from_behind(): return lax.ppermute(value, axis, pairs)  55.9 us
    dynamic_update_slice x2, local copies, waits for them, and re-layouts, shards(): lax.dynamic_update_slice(canvas, current + pictures[sub_index], (row_star...  7.04 us
    all_to_all x1, starting transfers between devices, shards(): lax.all_to_all(visibilities[0, 0], 'chan', split_axis=0, concat_axis=0, t...  6.32 us
    all_to_all x1, waiting for transfers between devices, shards(): lax.all_to_all(positions[0, 0], 'chan', split_axis=0, concat_axis=0, tile...  5.53 us
    all_to_all x1, starting transfers between devices, shards(): lax.all_to_all(positions[0, 0], 'chan', split_axis=0, concat_axis=0, tile...  5.1 us
    dot_general x2, matrix products, accumulate(): lax.dot_general(left_side, right_side, (((0,), (0,)), ((), ())), precisio...  4.21 us
    broadcast_in_dim x1, local copies, waits for them, and re-layouts, shards(): canvas = jnp.zeros((STRIP + grid_side, BAND + grid_side), jnp.float32)  4 us
    mul x2, other arithmetic, accumulate(): real_rows[:, None] * col_kernel  3.85 us
  transfers between devices with their start and end apart: 4, of which 3 were waited for; matrix products, arithmetic and copies ran while one was open for 6% of the time, Pallas kernels for 0%

commit v1 on v0

v1 whole, which is shorter than its diff:
```python
import functools
import math

import jax
import jax.numpy as jnp
import numpy as np
from jax import lax
from jax.experimental import pallas as pl
from jax.experimental.pallas import tpu as pltpu
from jax.sharding import PartitionSpec as P

TAPS = 8
STRIP = 256
BAND = 4096
SUB = 256
HALF = SUB // 2
BLOCK = 64
TILE = 16
LAST = BAND // SUB - 1


def real_basis():
    x = np.arange(SUB)
    rows = [np.cos(2 * np.pi * ((j * x) % SUB) / SUB) for j in range(HALF + 1)]
    rows += [np.sin(2 * np.pi * ((j * x) % SUB) / SUB) for j in range(1, HALF)]
    table = np.stack(rows).astype(np.float32)
    high = table.astype(jnp.bfloat16)
    low = (table - high.astype(np.float32)).astype(jnp.bfloat16)
    behind = np.concatenate([high, low, high], axis=0)
    ahead = np.concatenate([high.T, high.T, low.T], axis=1)
    return ahead, behind


def halves(value):
    high = value.astype(jnp.bfloat16)
    low = (value - high.astype(jnp.float32)).astype(jnp.bfloat16)
    return high, low


def taper(offset):
    angle = offset * (math.pi / TAPS)
    square = angle * angle
    series = jnp.float32(-1.0 / math.factorial(14))
    for order in range(12, -1, -2):
        sign = 1.0 if order % 4 == 0 else -1.0
        series = series * square + jnp.float32(sign / math.factorial(order))
    return jnp.where(jnp.abs(offset) < TAPS / 2, series * series, 0.0)


def folded(position, rho):
    base = jnp.floor(position) - (TAPS // 2 - 1)

    def cell_at(residue):
        ahead = residue - base
        ahead = ahead - TILE * jnp.floor(ahead * (1.0 / TILE))
        return base + ahead, ahead < TAPS

    cell, inside = cell_at(rho)
    direct = inside & (cell <= HALF)
    near = jnp.where(direct, taper(cell - position), 0.0)
    mirror, inside = cell_at(-rho)
    far = jnp.where(inside & (mirror > HALF), taper(mirror - position), 0.0)
    turn = jnp.where(direct, cell - rho, SUB - mirror - rho) * (1.0 / TILE)
    return near + far, near - far, turn.astype(jnp.bfloat16)


def fill_factors(n, me, tracks, counts, arrived, le, lo, we, wo):
    rows = arrived[0].shape[-1]
    depth = n * rows
    rho = lax.broadcasted_iota(jnp.int32, (TILE, rows), 0).astype(jnp.float32)
    lane_block = lax.broadcasted_iota(jnp.int32, (1, rows), 1) // BLOCK
    zero = jnp.zeros((TILE, rows), jnp.bfloat16)
    for k in range(n):
        source = lax.rem(me - k + n, n)
        live = lane_block < counts[0, 0, source]
        target = jnp.zeros((1, rows), jnp.int32)
        for b in range(rows // BLOCK):
            target = jnp.where(lane_block == b, tracks[0, 0, source, b], target)
        piece = arrived[k][...]
        real = jnp.where(live, piece[0:1], 0.0)
        imag = jnp.where(live, piece[1:2], 0.0)
        u_position = piece[2:3]
        u_even, u_odd, u_turn = folded(u_position, rho)
        v_even, v_odd, v_turn = folded(piece[3:4], rho)
        middle = taper(HALF - u_position)
        places = [(k * rows + part * depth) for part in range(3)]

        def put(ref, row, pair, order):
            for place, which in zip(places, order):
                ref[row : row + TILE, place : place + rows] = pair[which]

        left, right = (0, 1, 0), (0, 0, 1)
        first = target == 0
        evens = [halves(jnp.where(first, u_even, 0.0)), halves(jnp.where(first, 0.0, u_even))]
        odds = [halves(jnp.where(first, u_odd, 0.0)), halves(jnp.where(first, 0.0, u_odd))]
        for turn in range(HALF // TILE):
            chosen = u_turn == turn
            for s in range(2):
                row = s * HALF + turn * TILE
                put(le, row, [jnp.where(chosen, e, zero) for e in evens[s]], left)
                put(lo, row, [jnp.where(chosen, o, zero) for o in odds[s]], left)
        middles = jnp.where(
            (rho == 0) & first, middle, jnp.where((rho == 8) & jnp.logical_not(first), middle, 0.0)
        )
        put(le, 2 * HALF, halves(middles), left)
        for ref, cosine, sine in (
            (we, real * v_even, imag * v_odd),
            (wo, imag * v_even, -real * v_odd),
        ):
            cosine, sine = halves(cosine), halves(sine)
            for turn in range(HALF // TILE):
                chosen = v_turn == turn
                put(ref, turn * TILE, [jnp.where(chosen, c, zero) for c in cosine], right)
                pair = [jnp.where(chosen, c, zero) for c in sine]
                if turn == 0:
                    top = v_turn == HALF // TILE
                    pair = [jnp.where(top, c, p) for c, p in zip(cosine, pair)]
                put(ref, HALF + turn * TILE, pair, right)


def product(a, b, contract):
    return lax.dot_general(a, b, (contract, ((), ())), preferred_element_type=jnp.float32)


def picture_kernel(n, scale, tracks, counts, offsets, *refs):
    arrived = refs[:n]
    screens, ahead, behind, pictures, across, diagonal, le, lo, we, wo = refs[n:]
    me = lax.axis_index("chan")
    fill_factors(n, me, tracks, counts, arrived, le, lo, we, wo)
    even = product(le[...], we[...], ((1,), (1,)))
    odd = product(lo[...], wo[...], ((1,), (1,)))
    row_ids = lax.broadcasted_iota(jnp.int32, (SUB, SUB), 0)
    col_ids = lax.broadcasted_iota(jnp.int32, (SUB, SUB), 1)
    first_row = lax.broadcasted_iota(jnp.int32, (HALF, SUB), 0) == 0
    stays = jnp.zeros((SUB, SUB), jnp.float32)
    falls = jnp.zeros((SUB, SUB), jnp.float32)
    for s in range(2):
        middle = even[2 * HALF + 8 * s : 2 * HALF + 8 * s + 1]
        lower = jnp.where(first_row, middle, odd[s * HALF : (s + 1) * HALF])
        grid = jnp.concatenate([even[s * HALF : (s + 1) * HALF], lower], axis=0)
        high, low = halves(grid)
        half_way = product(
            jnp.concatenate([high, high, low], axis=1), behind[...], ((1,), (0,))
        )
        high, low = halves(half_way)
        image = product(ahead[...], jnp.concatenate([high, low, high], axis=0), ((1,), (0,)))
        image = screens[0, 0, s] * (image * scale)
        row = offsets[0, 0, s, 0]
        col = offsets[0, 0, s, 1]
        shift = lax.rem(col, SUB)
        image = pltpu.roll(pltpu.roll(image, row, 0), shift, 1)
        pictures[s] = image
        beyond = (col_ids < shift) & (col // SUB == LAST)
        stays = stays + jnp.where(beyond & (row_ids >= row), image, 0.0)
        falls = falls + jnp.where(beyond & (row_ids < row), image, 0.0)
    across[...] = stays
    diagonal[...] = falls


def paste_kernel(offsets, offsets_before, own, before, across, diagonal, out):
    out[...] = jnp.zeros_like(out)
    row_ids = lax.broadcasted_iota(jnp.int32, (SUB, SUB), 0)
    col_ids = lax.broadcasted_iota(jnp.int32, (SUB, SUB), 1)
    for pictures, corners, spilled in ((own, offsets, False), (before, offsets_before, True)):
        for s in range(2):
            row = corners[0, 0, s, 0]
            col = corners[0, 0, s, 1]
            shift = lax.rem(col, SUB)
            block = col // SUB
            here = (row_ids < row) if spilled else (row_ids >= row)
            image = jnp.where(here, pictures[s], 0.0)
            place = pl.ds(pl.multiple_of(block * SUB, SUB), SUB)
            out[:, place] += jnp.where(col_ids >= shift, image, 0.0)

            @pl.when(block < LAST)
            def _():
                place = pl.ds(pl.multiple_of((block + 1) * SUB, SUB), SUB)
                out[:, place] += jnp.where(col_ids < shift, image, 0.0)

    out[:, :SUB] += across[...] + diagonal[...]


def shards(mesh, visibilities, positions, tracks, counts, screens, offsets):
    n = mesh.shape["chan"]
    facets = mesh.shape["facet"]
    rows = visibilities.shape[-1]
    me = lax.axis_index("chan")
    vmem = pl.BlockSpec(memory_space=pltpu.VMEM)
    smem = pl.BlockSpec(memory_space=pltpu.SMEM)

    arrived = []
    for k in range(n):
        slot = lax.rem(me + k, n)
        piece = jnp.concatenate(
            [
                lax.dynamic_index_in_dim(visibilities[0, 0], slot, 0, keepdims=False),
                lax.dynamic_index_in_dim(positions[0, 0], slot, 0, keepdims=False),
            ],
            axis=0,
        )
        if k:
            piece = lax.ppermute(piece, "chan", [(i, (i + k) % n) for i in range(n)])
        arrived.append(piece)
    facet_ring = [(i, (i + 1) % facets) for i in range(facets)]
    offsets_before = lax.ppermute(offsets, "facet", facet_ring)

    ahead, behind = real_basis()
    depth = 3 * n * rows
    picture = jax.ShapeDtypeStruct((SUB, SUB), jnp.float32)
    pictures, across, diagonal = pl.pallas_call(
        functools.partial(picture_kernel, n, 1.0 / (2.0 * math.sqrt(n * rows))),
        out_shape=(jax.ShapeDtypeStruct((2, SUB, SUB), jnp.float32), picture, picture),
        in_specs=[smem] * 3 + [vmem] * (n + 3),
        out_specs=(vmem, vmem, vmem),
        scratch_shapes=[
            pltpu.VMEM((2 * HALF + TILE, depth), jnp.bfloat16),
            pltpu.VMEM((2 * HALF, depth), jnp.bfloat16),
            pltpu.VMEM((SUB, depth), jnp.bfloat16),
            pltpu.VMEM((SUB, depth), jnp.bfloat16),
        ],
        compiler_params=pltpu.CompilerParams(vmem_limit_bytes=56 * 1024 * 1024),
    )(tracks, counts, offsets, *arrived, screens, jnp.asarray(ahead), jnp.asarray(behind))

    before = lax.ppermute(pictures, "facet", facet_ring)
    across = lax.ppermute(across, "chan", [(i, (i + 1) % n) for i in range(n)])
    diagonal = lax.ppermute(
        diagonal,
        ("facet", "chan"),
        [
            (f * n + d, (f + 1) % facets * n + (d + 1) % n)
            for f in range(facets)
            for d in range(n)
        ],
    )
    return pl.pallas_call(
        paste_kernel,
        out_shape=jax.ShapeDtypeStruct((STRIP, BAND), jnp.float32),
        in_specs=[smem] * 2 + [vmem] * 4,
        out_specs=vmem,
        compiler_params=pltpu.CompilerParams(vmem_limit_bytes=56 * 1024 * 1024),
    )(offsets, offsets_before, pictures, before, across, diagonal)


def solution(mesh):
    return jax.shard_map(
        functools.partial(shards, mesh),
        mesh=mesh,
        in_specs=(
            P("facet", "chan", None, None, None),
            P("facet", "chan", None, None, None),
            P("facet", "chan", None, None),
            P("facet", "chan", None),
            P("facet", "chan", None, None, None),
            P("facet", "chan", None, None),
        ),
        out_specs=P("facet", "chan"),
        check_vma=False,
    )
```

time: 138 us -> 39.7 us (0.29)
  waiting for transfers between devices: 61.4 us -> 17.4 us
  matrix products: 21.8 us -> 0 us
  local copies, waits for them, and re-layouts: 19.1 us -> 3.46 us
  other arithmetic: 13.7 us -> 0.62 us
  Pallas kernels: 0 us -> 8.52 us
  between operations: 7.75 us -> 0.04 us
  starting transfers between devices: 12.6 us -> 9.55 us
    ppermute x2 -> x7, waiting for transfers between devices: 55.9 us -> 17.4 us  [the longest x1 8.14 us: shards(): offsets_before = lax.ppermute(offsets, 'facet', facet_ring)]
    dot_general x14 -> x0, matrix products: 21.8 us -> none  [the longest x2 4.21 us: accumulate(): lax.dot_general(left_side, right_side, (((0,), (0,)), ((), ())), precisio...]
    all_to_all x2 -> x0, starting transfers between devices: 11.4 us -> none  [the longest x1 6.32 us: shards(): lax.all_to_all(visibilities[0, 0], 'chan', split_axis=0, concat_axis=0, t...]
    pallas_call x0 -> x2, Pallas kernels: none -> 8.52 us  [the longest x1 4.58 us: shards(): pl.pallas_call(functools.partial(picture_kernel, n, 1.0 / (2.0 * math.sqr...]
    ppermute x2 -> x7, starting transfers between devices: 1.13 us -> 9.55 us  [the longest x3 7.93 us: shards(): piece = lax.ppermute(piece, 'chan', [(i, (i + k) % n) for i in range(n)])]
    dynamic_update_slice x2 -> x0, local copies, waits for them, and re-layouts: 7.04 us -> none  [shards(): lax.dynamic_update_slice(canvas, current + pictures[sub_index], (row_star...]
    slice x6 -> x0, local copies, waits for them, and re-layouts: 6.77 us -> none  [the longest x1 2.7 us: shards(): arrived_rows = from_behind(canvas[STRIP:], 'facet', 1)]
    all_to_all x2 -> x0, waiting for transfers between devices: 5.53 us -> none  [the longest x1 5.53 us: shards(): lax.all_to_all(positions[0, 0], 'chan', split_axis=0, concat_axis=0, tile...]
  transfers between devices with their start and end apart: 4 -> 7, of which waited for: 3 -> 4; matrix products, arithmetic and copies ran while one was open for 6% -> 2% of each run, Pallas kernels for 0% -> 0%
where the time goes in v1:
time: 39.7 us; the launch traced here: 39.6 us
  waiting for transfers between devices  17.4 us (44%)
  starting transfers between devices  9.55 us (24%)
  Pallas kernels  8.52 us (21%)
  local copies, waits for them, and re-layouts  3.46 us (9%)
  other arithmetic  0.62 us (2%)
    ppermute x1, waiting for transfers between devices, shards(): offsets_before = lax.ppermute(offsets, 'facet', facet_ring)  8.14 us
    ppermute x3, starting transfers between devices, shards(): piece = lax.ppermute(piece, 'chan', [(i, (i + k) % n) for i in range(n)])  7.93 us
    ppermute x1, waiting for transfers between devices, shards(): lax.ppermute(diagonal, ('facet', 'chan'), [(f * n + d, (f + 1) % facets *...  7.4 us
    pallas_call x1, Pallas kernels, shards(): pl.pallas_call(functools.partial(picture_kernel, n, 1.0 / (2.0 * math.sqr...  4.58 us
    pallas_call x1, Pallas kernels, shards(): pl.pallas_call(paste_kernel, out_shape=jax.ShapeDtypeStruct((STRIP, BAND)...  3.94 us
    unnamed x14, local copies, waits for them, and re-layouts  2.66 us
    ppermute x1, starting transfers between devices, shards(): lax.ppermute(diagonal, ('facet', 'chan'), [(f * n + d, (f + 1) % facets *...  1.5 us
    ppermute x3, waiting for transfers between devices, shards(): piece = lax.ppermute(piece, 'chan', [(i, (i + k) % n) for i in range(n)])  0.98 us
  transfers between devices with their start and end apart: 7, of which 4 were waited for; matrix products, arithmetic and copies ran while one was open for 2% of the time, Pallas kernels for 0%

profile of v1, /device:TPU:0, one launch (start us, length us, event | category | flops | bytes accessed | tf_op | source)
XLA Modules:
  0.0 39.6 jit_solution(241420537452025034)
XLA Ops:
  0.0 0.8 %dynamic-slice_bitcast_fusion = (f32[2,256]{1,0:T(2,128)S(1)}, f32[2,256]{1,0:T(2,128)S(1)}, f32[2,256]{1,0:T(2,128)S(1)}, f32[2,256]{1,0:T(2,128)S(1)}, f32[2,2...) fusion(f32[1,1,4,2,256]{4,3,2,1,0:T(2,128)} %param.9, s32[]{:T(128)S(6)} %select_n.20, ...), kind=kLoop, calls=%fused_computation.4 | loop fusion | bytes 32784 | tf_op jit(solution)/shard_map/jit(dynamic_index_in_dim)/squeeze | solution.py:197
  0.8 4.1 %collective-permute-start.2 = (f32[4,256]{1,0:T(4,128)S(1)}, f32[4,256]{1,0:T(4,128)S(1)}, u32[]{:S(2)}, u32[]{:S(2)}) collective-permute-start(f32[4,256]{1,0:T(4,128)S(1)} %pad_maximum_fusion.2), channel_id=1, source_target_pairs={{0,2},{1,3},{2,0},{3,1},{4,6},{5,7},{6,4},{7,5},{8,10},{9,11},{10,... | collective-permute-start | bytes 12296 | tf_op jit(solution)/shard_map/ppermute | solution.py:202
  4.9 1.6 %collective-permute-start.1 = (f32[4,256]{1,0:T(4,128)S(1)}, f32[4,256]{1,0:T(4,128)S(1)}, u32[]{:S(2)}, u32[]{:S(2)}) collective-permute-start(f32[4,256]{1,0:T(4,128)S(1)} %pad_maximum_fusion.1), channel_id=1, source_target_pairs={{0,1},{1,2},{2,3},{3,0},{4,5},{5,6},{6,7},{7,4},{8,9},{9,10},{10,1... | collective-permute-start | bytes 12296 | tf_op jit(solution)/shard_map/ppermute | solution.py:202
  6.5 2.2 %collective-permute-start.3 = (f32[4,256]{1,0:T(4,128)S(1)}, f32[4,256]{1,0:T(4,128)S(1)}, u32[]{:S(2)}, u32[]{:S(2)}) collective-permute-start(f32[4,256]{1,0:T(4,128)S(1)} %pad_maximum_fusion.3), channel_id=1, source_target_pairs={{0,3},{1,0},{2,1},{3,2},{4,7},{5,4},{6,5},{7,6},{8,11},{9,8},{10,9... | collective-permute-start | bytes 12296 | tf_op jit(solution)/shard_map/ppermute | solution.py:202
  8.8 0.6 %pad_maximum_fusion.refs_0_ = f32[4,256]{1,0:T(4,128)} fusion(f32[2,256]{1,0:T(2,128)S(1)} %get-tuple-element.17, f32[2,256]{1,0:T(2,128)S(1)} %get-tuple-element.20), kind=kLoop, calls=%fused_computation | loop fusion | flops 1024 | bytes 8192 | tf_op jit(solution)/shard_map/concatenate | solution.py:194
  9.3 0.0 collective-permute-done.2.refs_2_
  9.4 1.0 %collective-permute-done.1.refs_1_ = f32[4,256]{1,0:T(4,128)S(1)} collective-permute-done((f32[4,256]{1,0:T(4,128)S(1)}, f32[4,256]{1,0:T(4,128)S(1)}, u32[]{:S(2)}, u32[]{:S(2)}) %collective-permute-start.1) | collective-permute-done | bytes 4128 | tf_op jit(solution)/shard_map/ppermute | solution.py:202
  10.3 0.0 collective-permute-done.3.refs_3_
  10.3 0.0 copy-done.3
  10.3 0.6 %copy-done.4 = f32[4,256]{1,0:T(4,128)} copy-done((f32[4,256]{1,0:T(4,128)}, f32[4,256]{1,0:T(4,128)S(1)}, u32[]{:S(2)}) %copy-start.4) | copy-done | bytes 4120
  10.9 0.6 %copy-done.5 = f32[4,256]{1,0:T(4,128)} copy-done((f32[4,256]{1,0:T(4,128)}, f32[4,256]{1,0:T(4,128)S(1)}, u32[]{:S(2)}) %copy-start.5) | copy-done | bytes 4120
  11.5 4.6 %shard_map.82 = (f32[2,256,256]{2,1,0:T(8,128)}, f32[256,256]{1,0:T(8,128)}, f32[256,256]{1,0:T(8,128)}) custom-call(s32[1,1,4,4]{3,2,1,0:T(4,128)} %tracks.1, s32[1,1,4]{2,1,0:T(1,128)} %counts.1, s32[1,1,2,2]{3,2,1,0:T(2,128)} %offsets.3, f32[4,256]{1,0:T(4,128)} %pad_maximum_fusion.refs_0_, f32[4,256]{1,0:T(4,128)} %copy-done.4, f32[4,256]{1,0:T(4,128)} %copy-done.3, ...), custom_call_target="tpu_custom_call" | custom-call | tf_op jit(solution)/shard_map/pallas_call | solution.py:210
  16.1 0.0 collective-permute-start.4
  16.1 0.0 collective-permute-start.5
  16.1 1.5 %collective-permute-start.6 = (f32[256,256]{1,0:T(8,128)}, f32[256,256]{1,0:T(8,128)S(1)}, u32[]{:S(2)}, u32[]{:S(2)}) collective-permute-start(f32[256,256]{1,0:T(8,128)} %get-tuple-element.10), channel_id=1, source_target_pairs={{0,5},{1,6},{2,7},{3,4},{4,9},{5,10},{6,11},{7,8},{8,13},{9,14},{1... | collective-permute-start | bytes 786440 | tf_op jit(solution)/shard_map/ppermute | solution.py:226
  17.6 0.1 collective-permute-start
  17.7 8.1 %collective-permute-done.offsets_before = s32[1,1,2,2]{3,2,1,0:T(2,128)S(1)} collective-permute-done((s32[1,1,2,2]{3,2,1,0:T(2,128)}, s32[1,1,2,2]{3,2,1,0:T(2,128)S(1)}, u32[]{:S(2)}, u32[]{:S(2)}) %collective-permute-start) | collective-permute-done | bytes 48 | tf_op jit(solution)/shard_map/ppermute | solution.py:205
  25.9 0.9 %collective-permute-done.5.across = f32[256,256]{1,0:T(8,128)S(1)} collective-permute-done((f32[256,256]{1,0:T(8,128)}, f32[256,256]{1,0:T(8,128)S(1)}, u32[]{:S(2)}, u32[]{:S(2)}) %collective-permute-start.5) | collective-permute-done | bytes 262176 | tf_op jit(solution)/shard_map/ppermute | solution.py:225
  26.7 7.4 %collective-permute-done.6.diagonal = f32[256,256]{1,0:T(8,128)S(1)} collective-permute-done((f32[256,256]{1,0:T(8,128)}, f32[256,256]{1,0:T(8,128)S(1)}, u32[]{:S(2)}, u32[]{:S(2)}) %collective-permute-start.6) | collective-permute-done | bytes 262176 | tf_op jit(solution)/shard_map/ppermute | solution.py:226
  34.1 0.0 collective-permute-done.4.before
  34.1 0.0 copy-done.6
  34.1 0.7 %copy-done.2 = f32[256,256]{1,0:T(8,128)} copy-done((f32[256,256]{1,0:T(8,128)}, f32[256,256]{1,0:T(8,128)S(1)}, u32[]{:S(2)}) %copy-start.2) | copy-done | bytes 262168
  34.8 0.8 %copy-done = f32[2,256,256]{2,1,0:T(8,128)} copy-done((f32[2,256,256]{2,1,0:T(8,128)}, f32[2,256,256]{2,1,0:T(8,128)S(1)}, u32[]{:S(2)}) %copy-start) | copy-done | bytes 524312
  35.6 3.9 %shard_map.83 = f32[256,4096]{1,0:T(8,128)} custom-call(s32[1,1,2,2]{3,2,1,0:T(2,128)} %offsets.3, s32[1,1,2,2]{3,2,1,0:T(2,128)} %copy-done.6, f32[2,256,256]{2,1,0:T(8,128)} %get-tuple-element.8.own, f32[2,256,256]{2,1,0:T(8,128)} %copy-done, f32[256,256]{1,0:T(8,128)} %copy-done.1, f32[256,256]{1,0:T(8,128)} %copy-done.2), custom_call_target="tpu_custom_call" | custom-call | tf_op jit(solution)/shard_map/pallas_call | solution.py:235
  (11 shorter events, 0.0 us)
Async XLA Ops:
  0.8 8.5 %collective-permute-start.2 = (f32[4,256]{1,0:T(4,128)S(1)}, f32[4,256]{1,0:T(4,128)S(1)}, u32[]{:S(2)}, u32[]{:S(2)}) collective-permute-start(f32[4,256]{1,0:T(4,128)S(1)} %pad_maximum_fusion.2), channel_id=1, source_target_pairs={{0,2},{1,3},{2,0},{3,1},{4,6},{5,7},{6,4},{7,5},{8,10},{9,11},{10,... | collective-permute-start | bytes 12296 | tf_op jit(solution)/shard_map/ppermute | solution.py:202
  4.9 5.4 %collective-permute-start.1 = (f32[4,256]{1,0:T(4,128)S(1)}, f32[4,256]{1,0:T(4,128)S(1)}, u32[]{:S(2)}, u32[]{:S(2)}) collective-permute-start(f32[4,256]{1,0:T(4,128)S(1)} %pad_maximum_fusion.1), channel_id=1, source_target_pairs={{0,1},{1,2},{2,3},{3,0},{4,5},{5,6},{6,7},{7,4},{8,9},{9,10},{10,1... | collective-permute-start | bytes 12296 | tf_op jit(solution)/shard_map/ppermute | solution.py:202
  6.5 3.8 %collective-permute-start.3 = (f32[4,256]{1,0:T(4,128)S(1)}, f32[4,256]{1,0:T(4,128)S(1)}, u32[]{:S(2)}, u32[]{:S(2)}) collective-permute-start(f32[4,256]{1,0:T(4,128)S(1)} %pad_maximum_fusion.3), channel_id=1, source_target_pairs={{0,3},{1,0},{2,1},{3,2},{4,7},{5,4},{6,5},{7,6},{8,11},{9,8},{10,9... | collective-permute-start | bytes 12296 | tf_op jit(solution)/shard_map/ppermute | solution.py:202
  9.4 1.0 %copy-start.3 = (f32[4,256]{1,0:T(4,128)}, f32[4,256]{1,0:T(4,128)S(1)}, u32[]{:S(2)}) copy-start(f32[4,256]{1,0:T(4,128)S(1)} %collective-permute-done.2.refs_2_) | copy-start | bytes 12292
  10.3 0.6 %copy-start.4 = (f32[4,256]{1,0:T(4,128)}, f32[4,256]{1,0:T(4,128)S(1)}, u32[]{:S(2)}) copy-start(f32[4,256]{1,0:T(4,128)S(1)} %collective-permute-done.1.refs_1_) | copy-start | bytes 12292
  10.9 0.6 %copy-start.5 = (f32[4,256]{1,0:T(4,128)}, f32[4,256]{1,0:T(4,128)S(1)}, u32[]{:S(2)}) copy-start(f32[4,256]{1,0:T(4,128)S(1)} %collective-permute-done.3.refs_3_) | copy-start | bytes 12292
  16.1 18.0 %collective-permute-start.4 = (f32[2,256,256]{2,1,0:T(8,128)}, f32[2,256,256]{2,1,0:T(8,128)S(1)}, u32[]{:S(2)}, u32[]{:S(2)}) collective-permute-start(f32[2,256,256]{2,1,0:T(8,128)} %get-tuple-element.8.own), channel_id=1, source_target_pairs={{0,4},{4,8},{8,12},{12,16},{16,20},{20,24},{24,28},{28,0},{1,5},{5... | collective-permute-start | bytes 1572872 | tf_op jit(solution)/shard_map/ppermute | solution.py:224
  16.1 10.6 %collective-permute-start.5 = (f32[256,256]{1,0:T(8,128)}, f32[256,256]{1,0:T(8,128)S(1)}, u32[]{:S(2)}, u32[]{:S(2)}) collective-permute-start(f32[256,256]{1,0:T(8,128)} %get-tuple-element.9), channel_id=1, source_target_pairs={{0,1},{1,2},{2,3},{3,0},{4,5},{5,6},{6,7},{7,4},{8,9},{9,10},{10,1... | collective-permute-start | bytes 786440 | tf_op jit(solution)/shard_map/ppermute | solution.py:225
  16.1 18.0 %collective-permute-start.6 = (f32[256,256]{1,0:T(8,128)}, f32[256,256]{1,0:T(8,128)S(1)}, u32[]{:S(2)}, u32[]{:S(2)}) collective-permute-start(f32[256,256]{1,0:T(8,128)} %get-tuple-element.10), channel_id=1, source_target_pairs={{0,5},{1,6},{2,7},{3,4},{4,9},{5,10},{6,11},{7,8},{8,13},{9,14},{1... | collective-permute-start | bytes 786440 | tf_op jit(solution)/shard_map/ppermute | solution.py:226
  17.6 8.3 %collective-permute-start = (s32[1,1,2,2]{3,2,1,0:T(2,128)}, s32[1,1,2,2]{3,2,1,0:T(2,128)S(1)}, u32[]{:S(2)}, u32[]{:S(2)}) collective-permute-start(s32[1,1,2,2]{3,2,1,0:T(2,128)} %offsets.3), channel_id=1, source_target_pairs={{0,4},{4,8},{8,12},{12,16},{16,20},{20,24},{24,28},{28,0},{1,5},{5... | collective-permute-start | bytes 56 | tf_op jit(solution)/shard_map/ppermute | solution.py:205
  25.8 8.3 %copy-start.6 = (s32[1,1,2,2]{3,2,1,0:T(2,128)}, s32[1,1,2,2]{3,2,1,0:T(2,128)S(1)}, u32[]{:S(2)}) copy-start(s32[1,1,2,2]{3,2,1,0:T(2,128)S(1)} %collective-permute-done.offsets_before) | copy-start | bytes 52
  26.7 7.4 %copy-start.1 = (f32[256,256]{1,0:T(8,128)}, f32[256,256]{1,0:T(8,128)S(1)}, u32[]{:S(2)}) copy-start(f32[256,256]{1,0:T(8,128)S(1)} %collective-permute-done.5.across) | copy-start | bytes 786436
  34.1 0.7 %copy-start.2 = (f32[256,256]{1,0:T(8,128)}, f32[256,256]{1,0:T(8,128)S(1)}, u32[]{:S(2)}) copy-start(f32[256,256]{1,0:T(8,128)S(1)} %collective-permute-done.6.diagonal) | copy-start | bytes 786436
  34.8 0.8 %copy-start = (f32[2,256,256]{2,1,0:T(8,128)}, f32[2,256,256]{2,1,0:T(8,128)S(1)}, u32[]{:S(2)}) copy-start(f32[2,256,256]{2,1,0:T(8,128)S(1)} %collective-permute-done.4.before) | copy-start | bytes 1572868

commit v2 on v1

v2 whole, which is shorter than its diff:
```python
import functools
import math

import jax
import jax.numpy as jnp
from jax import lax
from jax.experimental import pallas as pl
from jax.experimental.pallas import tpu as pltpu
from jax.sharding import PartitionSpec as P

TAPS = 8
STRIP = 256
BAND = 4096
SUB = 256
HALF = SUB // 2
BLOCK = 64
TILE = 16
LAST = BAND // SUB - 1


def tables_kernel(ahead, behind):
    shape = (SUB, SUB)
    for across, out in ((1, ahead), (0, behind)):
        j = lax.broadcasted_iota(jnp.int32, shape, across)
        x = lax.broadcasted_iota(jnp.int32, shape, 1 - across)
        turn = jnp.where(j > HALF, (j - HALF) * x + 3 * SUB // 4, j * x) & (SUB - 1)
        turn = jnp.minimum(turn, SUB - turn).astype(jnp.float32)
        half_angle = cosine(turn * (math.pi / SUB))
        high, low = halves(2.0 * half_angle * half_angle - 1.0)
        parts = (high, high, low) if across else (high, low, high)
        out[...] = jnp.concatenate(parts, axis=across)


def halves(value):
    high = value.astype(jnp.bfloat16)
    low = (value - high.astype(jnp.float32)).astype(jnp.bfloat16)
    return high, low


def cosine(angle):
    square = angle * angle
    series = jnp.float32(-1.0 / math.factorial(14))
    for order in range(12, -1, -2):
        sign = 1.0 if order % 4 == 0 else -1.0
        series = series * square + jnp.float32(sign / math.factorial(order))
    return series


def taper(offset):
    series = cosine(offset * (math.pi / TAPS))
    return jnp.where(jnp.abs(offset) < TAPS / 2, series * series, 0.0)


def folded(position, rho):
    base = jnp.floor(position) - (TAPS // 2 - 1)

    def cell_at(residue):
        ahead = residue - base
        ahead = ahead - TILE * jnp.floor(ahead * (1.0 / TILE))
        return base + ahead, ahead < TAPS

    cell, inside = cell_at(rho)
    direct = inside & (cell <= HALF)
    near = jnp.where(direct, taper(cell - position), 0.0)
    mirror, inside = cell_at(-rho)
    far = jnp.where(inside & (mirror > HALF), taper(mirror - position), 0.0)
    turn = jnp.where(direct, cell - rho, SUB - mirror - rho) * (1.0 / TILE)
    return near + far, near - far, turn.astype(jnp.bfloat16)


def pack_kernel(n, tracks, counts, offsets, visibilities, positions, *outs):
    me = lax.axis_index("chan")
    base = outs[n - 1]
    base[...] = jnp.zeros_like(base)
    for k in range(n):
        slot = lax.rem(me + k, n)
        out = outs[k - 1] if k else base.at[0]
        out[0:2] = visibilities[0, 0, slot]
        out[2:4] = positions[0, 0, slot]
    capacity = tracks.shape[-1]
    values = [tracks[0, 0, c, b] for c in range(n) for b in range(capacity)]
    values += [counts[0, 0, c] for c in range(n)]
    values += [offsets[0, 0, s, axis] for s in range(2) for axis in range(2)]
    lane = lax.broadcasted_iota(jnp.int32, base.shape[1:], 1)
    numbers = jnp.zeros(lane.shape, jnp.int32)
    for place, value in enumerate(values):
        numbers = jnp.where(lane == place, value, numbers)
    base[1] = numbers.astype(jnp.float32)


def fill_factors(n, me, numbers, pieces, le, lo, we, wo):
    rows = pieces.shape[-1]
    depth = n * rows
    capacity = rows // BLOCK
    rho = lax.broadcasted_iota(jnp.int32, (TILE, rows), 0).astype(jnp.float32)
    lane_block = lax.broadcasted_iota(jnp.int32, (1, rows), 1) // BLOCK
    zero = jnp.zeros((TILE, rows), jnp.bfloat16)
    for k in range(n):
        source = lax.rem(me - k + n, n)
        live = lane_block.astype(jnp.float32) < numbers[0, n * capacity + source]
        target = jnp.zeros((1, rows), jnp.float32)
        for b in range(capacity):
            target = jnp.where(lane_block == b, numbers[0, source * capacity + b], target)
        piece = pieces[k + 1 if k else 0]
        real = jnp.where(live, piece[0:1], 0.0)
        imag = jnp.where(live, piece[1:2], 0.0)
        u_position = piece[2:3]
        u_even, u_odd, u_turn = folded(u_position, rho)
        v_even, v_odd, v_turn = folded(piece[3:4], rho)
        middle = taper(HALF - u_position)
        places = [(k * rows + part * depth) for part in range(3)]

        def put(ref, row, pair, order):
            for place, which in zip(places, order):
                ref[row : row + TILE, place : place + rows] = pair[which]

        left, right = (0, 1, 0), (0, 0, 1)
        first = target == 0.0
        evens = [halves(jnp.where(first, u_even, 0.0)), halves(jnp.where(first, 0.0, u_even))]
        odds = [halves(jnp.where(first, u_odd, 0.0)), halves(jnp.where(first, 0.0, u_odd))]
        for turn in range(HALF // TILE):
            chosen = u_turn == turn
            for s in range(2):
                row = s * HALF + turn * TILE
                put(le, row, [jnp.where(chosen, e, zero) for e in evens[s]], left)
                put(lo, row, [jnp.where(chosen, o, zero) for o in odds[s]], left)
        middles = jnp.where(
            (rho == 0) & first, middle, jnp.where((rho == 8) & jnp.logical_not(first), middle, 0.0)
        )
        put(le, 2 * HALF, halves(middles), left)
        for ref, cosine, sine in (
            (we, real * v_even, imag * v_odd),
            (wo, imag * v_even, -real * v_odd),
        ):
            cosine, sine = halves(cosine), halves(sine)
            for turn in range(HALF // TILE):
                chosen = v_turn == turn
                put(ref, turn * TILE, [jnp.where(chosen, c, zero) for c in cosine], right)
                pair = [jnp.where(chosen, c, zero) for c in sine]
                if turn == 0:
                    top = v_turn == HALF // TILE
                    pair = [jnp.where(top, c, p) for c, p in zip(cosine, pair)]
                put(ref, HALF + turn * TILE, pair, right)


def product(a, b, contract):
    return lax.dot_general(a, b, (contract, ((), ())), preferred_element_type=jnp.float32)


def picture_kernel(n, scale, spilled, *refs):
    count = 5 if spilled else 4
    payload_in, screens_in, ahead_in, behind_in = refs[:4]
    pictures, across = refs[count : count + 2]
    pieces, numbers, screens, ahead, behind, le, lo, we, wo, sems = refs[count + 2 :]
    copies = [
        pltpu.make_async_copy(source, target, sems.at[i])
        for i, (source, target) in enumerate(
            (
                (payload_in.at[1, pl.ds(0, 1)], numbers),
                (payload_in, pieces),
                (behind_in, behind),
                (ahead_in, ahead),
                (screens_in.at[0, 0], screens),
            )
        )
    ]
    for copy in copies:
        copy.start()
    copies[0].wait()
    copies[1].wait()
    me = lax.axis_index("chan")
    fill_factors(n, me, numbers, pieces, le, lo, we, wo)
    even = product(le[...], we[...], ((1,), (1,)))
    odd = product(lo[...], wo[...], ((1,), (1,)))
    copies[2].wait()
    copies[3].wait()
    copies[4].wait()
    row_ids = lax.broadcasted_iota(jnp.int32, (SUB, SUB), 0)
    col_ids = lax.broadcasted_iota(jnp.int32, (SUB, SUB), 1)
    first_row = lax.broadcasted_iota(jnp.int32, (HALF, SUB), 0) == 0
    total = refs[4][...] if spilled else jnp.zeros((SUB, SUB), jnp.float32)
    corner = n * (pieces.shape[-1] // BLOCK + 1)
    for s in range(2):
        middle = even[2 * HALF + 8 * s : 2 * HALF + 8 * s + 1]
        lower = jnp.where(first_row, middle, odd[s * HALF : (s + 1) * HALF])
        grid = jnp.concatenate([even[s * HALF : (s + 1) * HALF], lower], axis=0)
        high, low = halves(grid)
        half_way = product(
            jnp.concatenate([high, high, low], axis=1), behind[...], ((1,), (0,))
        )
        high, low = halves(half_way)
        image = product(ahead[...], jnp.concatenate([high, low, high], axis=0), ((1,), (0,)))
        image = screens[s] * (image * scale)
        row = numbers[0, corner + 2 * s].astype(jnp.int32)
        col = numbers[0, corner + 2 * s + 1].astype(jnp.int32)
        shift = lax.rem(col, SUB)
        image = pltpu.roll(pltpu.roll(image, row, 0), shift, 1)
        here = (row_ids < row) if spilled else (row_ids >= row)
        image = jnp.where(here, image, 0.0)
        pictures[s] = image
        beyond = (col_ids < shift) & (col // SUB == LAST)
        total = total + jnp.where(beyond, image, 0.0)
    across[...] = total


def paste_kernel(n, corner, payload_in, payload_before, own, before, out, numbers, sems):
    copies = [
        pltpu.make_async_copy(source.at[1, pl.ds(0, 1)], numbers.at[pl.ds(i, 1)], sems.at[i])
        for i, source in enumerate((payload_in, payload_before))
    ]
    for copy in copies:
        copy.start()
    out[...] = jnp.zeros_like(out)
    for copy in copies:
        copy.wait()
    col_ids = lax.broadcasted_iota(jnp.int32, (SUB, SUB), 1)
    for i, pictures in enumerate((own, before)):
        for s in range(2):
            col = numbers[i, corner + 2 * s + 1].astype(jnp.int32)
            shift = lax.rem(col, SUB)
            block = col // SUB
            image = pictures[s]
            place = pl.ds(pl.multiple_of(block * SUB, SUB), SUB)
            out[:, place] += jnp.where(col_ids >= shift, image, 0.0)

            @pl.when(block < LAST)
            def _():
                place = pl.ds(pl.multiple_of((block + 1) * SUB, SUB), SUB)
                out[:, place] += jnp.where(col_ids < shift, image, 0.0)


def finish_kernel(image_in, across_in, image_out, block, across, sems):
    window = pl.ds(0, SUB)
    copies = [
        pltpu.make_async_copy(image_in.at[:, window], block, sems.at[0]),
        pltpu.make_async_copy(across_in, across, sems.at[1]),
    ]
    for copy in copies:
        copy.start()
    for copy in copies:
        copy.wait()
    block[...] += across[...]
    copy = pltpu.make_async_copy(block, image_out.at[:, window], sems.at[2])
    copy.start()
    copy.wait()


def shards(mesh, visibilities, positions, tracks, counts, screens, offsets):
    n = mesh.shape["chan"]
    facets = mesh.shape["facet"]
    rows = visibilities.shape[-1]
    vmem = pl.BlockSpec(memory_space=pltpu.VMEM)
    anywhere = pl.BlockSpec(memory_space=pl.ANY)
    hbm = pl.BlockSpec(memory_space=pltpu.HBM)
    facet_ring = [(i, (i + 1) % facets) for i in range(facets)]

    packed = pl.pallas_call(
        functools.partial(pack_kernel, n),
        out_shape=(jax.ShapeDtypeStruct((4, rows), jnp.float32),) * (n - 1)
        + (jax.ShapeDtypeStruct((2, 4, rows), jnp.float32),),
        in_specs=[pl.BlockSpec(memory_space=pltpu.SMEM)] * 3 + [vmem] * 2,
        out_specs=(vmem,) * n,
        compiler_params=pltpu.CompilerParams(vmem_limit_bytes=56 << 20),
    )(tracks, counts, offsets, visibilities, positions)
    arrived = [
        lax.ppermute(packed[k - 1], "chan", [(i, (i + k) % n) for i in range(n)])
        for k in range(1, n)
    ]
    screens_before = lax.ppermute(screens, "facet", facet_ring)
    base, screens_before = lax.optimization_barrier((packed[n - 1], screens_before))
    payload = jnp.concatenate([base] + [piece[None] for piece in arrived], axis=0)
    payload = jnp.pad(payload, ((0, 0), (0, 4), (0, 0)))
    payload_before = lax.ppermute(payload, "facet", facet_ring)

    ahead, behind = pl.pallas_call(
        tables_kernel,
        out_shape=(
            jax.ShapeDtypeStruct((SUB, 3 * SUB), jnp.bfloat16),
            jax.ShapeDtypeStruct((3 * SUB, SUB), jnp.bfloat16),
        ),
        out_specs=(vmem, vmem),
        compiler_params=pltpu.CompilerParams(vmem_limit_bytes=8 << 20),
        cost_estimate=pl.CostEstimate(flops=4 << 20, bytes_accessed=1 << 20, transcendentals=0),
    )()
    depth = 3 * n * rows
    picture = jax.ShapeDtypeStruct((SUB, SUB), jnp.float32)
    scale = 1.0 / (2.0 * math.sqrt(n * rows))
    factor_rows = 4 * HALF + TILE + 2 * SUB
    room = 24 + (2 * factor_rows * depth >> 20)

    def pictures_of(spilled, *operands):
        return pl.pallas_call(
            functools.partial(picture_kernel, n, scale, spilled),
            out_shape=(jax.ShapeDtypeStruct((2, SUB, SUB), jnp.float32), picture),
            in_specs=[anywhere] * 4
            + [vmem] * (len(operands) - 4),
            out_specs=(vmem, vmem),
            scratch_shapes=[
                pltpu.VMEM((n + 1, 8, rows), jnp.float32),
                pltpu.SMEM((1, rows), jnp.float32),
                pltpu.VMEM((2, SUB, SUB), jnp.float32),
                pltpu.VMEM(ahead.shape, jnp.bfloat16),
                pltpu.VMEM(behind.shape, jnp.bfloat16),
                pltpu.VMEM((2 * HALF + TILE, depth), jnp.bfloat16),
                pltpu.VMEM((2 * HALF, depth), jnp.bfloat16),
                pltpu.VMEM((SUB, depth), jnp.bfloat16),
                pltpu.VMEM((SUB, depth), jnp.bfloat16),
                pltpu.SemaphoreType.DMA((5,)),
            ],
            compiler_params=pltpu.CompilerParams(vmem_limit_bytes=max(room, 0 if spilled else 52) << 20),
            cost_estimate=pl.CostEstimate(
                flops=2 * depth * SUB * SUB * 4, bytes_accessed=4 << 20, transcendentals=0
            ),
        )(*operands)

    own, across = pictures_of(False, payload, screens, ahead, behind)
    before, across = pictures_of(True, payload_before, screens_before, ahead, behind, across)
    across = lax.ppermute(across, "chan", [(i, (i + 1) % n) for i in range(n)])
    image = pl.pallas_call(
        functools.partial(paste_kernel, n, n * (rows // BLOCK + 1)),
        out_shape=jax.ShapeDtypeStruct((STRIP, BAND), jnp.float32),
        in_specs=[anywhere] * 2 + [vmem] * 2,
        out_specs=vmem,
        scratch_shapes=[pltpu.SMEM((2, rows), jnp.float32), pltpu.SemaphoreType.DMA((2,))],
        compiler_params=pltpu.CompilerParams(vmem_limit_bytes=16 << 20),
        cost_estimate=pl.CostEstimate(flops=1 << 20, bytes_accessed=12 << 20, transcendentals=0),
    )(payload, payload_before, own, before)
    return pl.pallas_call(
        finish_kernel,
        out_shape=jax.ShapeDtypeStruct((STRIP, BAND), jnp.float32),
        in_specs=[anywhere] * 2,
        out_specs=anywhere,
        scratch_shapes=[
            pltpu.VMEM((STRIP, SUB), jnp.float32),
            pltpu.VMEM((STRIP, SUB), jnp.float32),
            pltpu.SemaphoreType.DMA((3,)),
        ],
        input_output_aliases={0: 0},
        compiler_params=pltpu.CompilerParams(vmem_limit_bytes=4 << 20),
    )(image, across)


def solution(mesh):
    return jax.shard_map(
        functools.partial(shards, mesh),
        mesh=mesh,
        in_specs=(
            P("facet", "chan", None, None, None),
            P("facet", "chan", None, None, None),
            P("facet", "chan", None, None),
            P("facet", "chan", None),
            P("facet", "chan", None, None, None),
            P("facet", "chan", None, None),
        ),
        out_specs=P("facet", "chan"),
        check_vma=False,
    )
```

time: 39.7 us -> 31 us (0.78)
  waiting for transfers between devices: 17.4 us -> 8.71 us
  Pallas kernels: 8.52 us -> 12.2 us
  local copies, waits for them, and re-layouts: 3.46 us -> 0 us
  starting transfers between devices: 9.55 us -> 9.14 us
    ppermute x6 -> x5, waiting for transfers between devices: 16.5 us -> 3.28 us  [the longest x1 1.6 us: shards(): screens_before = lax.ppermute(screens, 'facet', facet_ring)]
    ppermute x1, waiting for transfers between devices: 0.85 us -> 5.43 us  [shards(): across = lax.ppermute(across, 'chan', [(i, (i + 1) % n) for i in range(n)])]
    pallas_call x2 -> x6, Pallas kernels: 8.52 us -> 12.2 us  [the longest x2 5.84 us: pictures_of(): pl.pallas_call(functools.partial(picture_kernel, n, scale, spilled), out_...]
    unnamed x14 -> x0, local copies, waits for them, and re-layouts: 2.66 us -> none
    ppermute x6 -> x5, starting transfers between devices: 9.54 us -> 7.13 us  [the longest x3 6.51 us: shards(): lax.ppermute(packed[k - 1], 'chan', [(i, (i + k) % n) for i in range(n)])]
    ppermute x1, starting transfers between devices: 0.01 us -> 2.01 us  [shards(): across = lax.ppermute(across, 'chan', [(i, (i + 1) % n) for i in range(n)])]
    squeeze x1 -> x0, local copies, waits for them, and re-layouts: 0.8 us -> none  [shards(): lax.dynamic_index_in_dim(positions[0, 0], slot, 0, keepdims=False)]
  transfers between devices with their start and end apart: 7 -> 6, of which waited for: 4 -> 4; matrix products, arithmetic and copies ran while one was open for 2% -> 0% of each run, Pallas kernels for 0% -> 25%
where the time goes in v2:
time: 31 us; the launch traced here: 30.8 us
  Pallas kernels  12.2 us (39%)
  starting transfers between devices  9.14 us (29%)
  waiting for transfers between devices  8.71 us (28%)
  other arithmetic  0.71 us (2%)
    ppermute x3, starting transfers between devices, shards(): lax.ppermute(packed[k - 1], 'chan', [(i, (i + k) % n) for i in range(n)])  6.51 us
    pallas_call x2, Pallas kernels, pictures_of(): pl.pallas_call(functools.partial(picture_kernel, n, scale, spilled), out_...  5.84 us
    ppermute x1, waiting for transfers between devices, shards(): across = lax.ppermute(across, 'chan', [(i, (i + 1) % n) for i in range(n)])  5.43 us
    pallas_call x1, Pallas kernels, shards(): pl.pallas_call(functools.partial(paste_kernel, n, n * (rows // BLOCK + 1)...  2.83 us
    ppermute x1, starting transfers between devices, shards(): across = lax.ppermute(across, 'chan', [(i, (i + 1) % n) for i in range(n)])  2.01 us
    pallas_call x1, Pallas kernels, shards(): pl.pallas_call(finish_kernel, out_shape=jax.ShapeDtypeStruct((STRIP, BAND...  1.71 us
    ppermute x1, waiting for transfers between devices, shards(): screens_before = lax.ppermute(screens, 'facet', facet_ring)  1.6 us
    pallas_call x1, Pallas kernels, shards(): pl.pallas_call(functools.partial(pack_kernel, n), out_shape=(jax.ShapeDty...  1.36 us
  transfers between devices with their start and end apart: 6, of which 4 were waited for; matrix products, arithmetic and copies ran while one was open for 0% of the time, Pallas kernels for 25%

profile of v2, /device:TPU:0, one launch (start us, length us, event | category | flops | bytes accessed | tf_op | source)
XLA Modules:
  0.0 30.8 jit_solution(3059472875384234030)
XLA Ops:
  0.0 0.5 %collective-permute-start = (f32[1,1,2,256,256]{4,3,2,1,0:T(8,128)}, f32[1,1,2,256,256]{4,3,2,1,0:T(8,128)S(1)}, u32[]{:S(2)}, u32[]{:S(2)}) collective-permute-start(f32[1,1,2,256,256]{4,3,2,1,0:T(8,128)} %refs_1_.1), channel_id=1, source_target_pairs={{0,4},{4,8},{8,12},{12,16},{16,20},{20,24},{24,28},{28,0},{1,5},{5... | collective-permute-start | bytes 1572872 | tf_op jit(solution)/shard_map/ppermute | solution.py:269
  0.5 1.4 %shard_map.64 = (f32[4,256]{1,0:T(4,128)}, f32[4,256]{1,0:T(4,128)}, f32[4,256]{1,0:T(4,128)}, f32[2,4,256]{2,1,0:T(4,128)}) custom-call(s32[1,1,4,4]{3,2,1,0:T(4,128)} %tracks.1, s32[1,1,4]{2,1,0:T(1,128)} %counts.1, s32[1,1,2,2]{3,2,1,0:T(2,128)} %offsets.1, f32[1,1,4,2,256]{4,3,2,1,0:T(2,128)} %visibilities.1, f32[1,1,4,2,256]{4,3,2,1,0:T(2,128)} %positions.1), custom_call_target="tpu_custom_call" | custom-call | tf_op jit(solution)/shard_map/pallas_call | solution.py:257
  1.8 2.6 %collective-permute-start.1 = (f32[4,256]{1,0:T(4,128)}, f32[4,256]{1,0:T(4,128)S(1)}, u32[]{:S(2)}, u32[]{:S(2)}) collective-permute-start(f32[4,256]{1,0:T(4,128)} %get-tuple-element.19), channel_id=1, source_target_pairs={{0,1},{1,2},{2,3},{3,0},{4,5},{5,6},{6,7},{7,4},{8,9},{9,10},{10,1... | collective-permute-start | bytes 12296 | tf_op jit(solution)/shard_map/ppermute | solution.py:266
  4.4 2.6 %collective-permute-start.2 = (f32[4,256]{1,0:T(4,128)}, f32[4,256]{1,0:T(4,128)S(1)}, u32[]{:S(2)}, u32[]{:S(2)}) collective-permute-start(f32[4,256]{1,0:T(4,128)} %get-tuple-element.20), channel_id=1, source_target_pairs={{0,2},{1,3},{2,0},{3,1},{4,6},{5,7},{6,4},{7,5},{8,10},{9,11},{10,... | collective-permute-start | bytes 12296 | tf_op jit(solution)/shard_map/ppermute | solution.py:266
  7.0 1.3 %collective-permute-start.3 = (f32[4,256]{1,0:T(4,128)}, f32[4,256]{1,0:T(4,128)S(1)}, u32[]{:S(2)}, u32[]{:S(2)}) collective-permute-start(f32[4,256]{1,0:T(4,128)} %get-tuple-element.21), channel_id=1, source_target_pairs={{0,3},{1,0},{2,1},{3,2},{4,7},{5,4},{6,5},{7,6},{8,11},{9,8},{10,9... | collective-permute-start | bytes 12296 | tf_op jit(solution)/shard_map/ppermute | solution.py:266
  8.3 0.5 %shard_map.65 = (bf16[256,768]{1,0:T(8,128)(2,1)S(1)}, bf16[768,256]{1,0:T(8,128)(2,1)S(1)}) custom-call(), custom_call_target="tpu_custom_call" | custom-call | flops 4194304 | bytes 1048576 | tf_op jit(solution)/shard_map/pallas_call | solution.py:275
  8.8 1.6 %collective-permute-done.refs_1_ = f32[1,1,2,256,256]{4,3,2,1,0:T(8,128)S(1)} collective-permute-done((f32[1,1,2,256,256]{4,3,2,1,0:T(8,128)}, f32[1,1,2,256,256]{4,3,2,1,0:T(8,128)S(1)}, u32[]{:S(2)}, u32[]{:S(2)}) %collective-permute-start) | collective-permute-done | bytes 524320 | tf_op jit(solution)/shard_map/ppermute | solution.py:269
  10.4 0.0 collective-permute-done.1
  10.4 0.0 collective-permute-done.2
  10.4 0.4 %collective-permute-done.3 = f32[4,256]{1,0:T(4,128)S(1)} collective-permute-done((f32[4,256]{1,0:T(4,128)}, f32[4,256]{1,0:T(4,128)S(1)}, u32[]{:S(2)}, u32[]{:S(2)}) %collective-permute-start.3) | collective-permute-done | bytes 4128 | tf_op jit(solution)/shard_map/ppermute | solution.py:266
  10.8 0.7 %select_maximum_fusion.refs_0_.payload_in = f32[5,8,256]{2,1,0:T(8,128)S(1)} fusion(f32[1,4,256]{2,1,0:T(4,128)S(1)} %bitcast.5, f32[1,4,256]{2,1,0:T(4,128)S(1)} %bitcast.4, f32[1,4,256]{2,1,0:T(4,128)S(1)} %bitcast.3, f32[2,4,256]{2,1,0:T(4,128)} %get-tuple-element.18), kind=kLoop, calls=%fused_computation | loop fusion | flops 81920 | bytes 61440 | tf_op jit(solution)/shard_map/concatenate | solution.py:271
  11.5 0.2 collective-permute-start.4
  11.7 2.9 %shard_map.66 = (f32[2,256,256]{2,1,0:T(8,128)S(1)}, f32[256,256]{1,0:T(8,128)S(1)}) custom-call(f32[5,8,256]{2,1,0:T(8,128)S(1)} %select_maximum_fusion.refs_0_.payload_in, f32[1,1,2,256,256]{4,3,2,1,0:T(8,128)} %refs_1_.1, bf16[256,768]{1,0:T(8,128)(2,1)S(1)} %get-tuple-element.22.refs_2_, bf16[768,256]{1,0:T(8,128)(2,1)S(1)} %get-tuple-element.23.refs_3_), custom_call_target="tpu_custom_call" | custom-call | flops 1610612736 | bytes 4194304 | tf_op jit(solution)/shard_map/pallas_call | solution.py:292
  14.6 1.3 %collective-permute-done.4.refs_0_.payload_before = f32[5,8,256]{2,1,0:T(8,128)S(1)} collective-permute-done((f32[5,8,256]{2,1,0:T(8,128)S(1)}, f32[5,8,256]{2,1,0:T(8,128)S(1)}, u32[]{:S(2)}, u32[]{:S(2)}) %collective-permute-start.4) | collective-permute-done | bytes 40992 | tf_op jit(solution)/shard_map/ppermute | solution.py:273
  15.9 2.9 %shard_map.67 = (f32[2,256,256]{2,1,0:T(8,128)S(1)}, f32[256,256]{1,0:T(8,128)S(1)}) custom-call(f32[5,8,256]{2,1,0:T(8,128)S(1)} %collective-permute-done.4.refs_0_.payload_before, f32[1,1,2,256,256]{4,3,2,1,0:T(8,128)S(1)} %collective-permute-done.refs_1_, bf16[256,768]{1,0:T(8,128)(2,1)S(1)} %get-tuple-element.22.refs_2_, ...), custom_call_target="tpu_custom_call" | custom-call | flops 1610612736 | bytes 4194304 | tf_op jit(solution)/shard_map/pallas_call | solution.py:292
  18.8 2.0 %collective-permute-start.5 = (f32[256,256]{1,0:T(8,128)S(1)}, f32[256,256]{1,0:T(8,128)S(1)}, u32[]{:S(2)}, u32[]{:S(2)}) collective-permute-start(f32[256,256]{1,0:T(8,128)S(1)} %get-tuple-element.28), channel_id=1, source_target_pairs={{0,1},{1,2},{2,3},{3,0},{4,5},{5,6},{6,7},{7,4},{8,9},{9,10},{10,1... | collective-permute-start | bytes 786440 | tf_op jit(solution)/shard_map/ppermute | solution.py:318
  20.8 2.8 %shard_map.68.image_in = f32[256,4096]{1,0:T(8,128)} custom-call(f32[5,8,256]{2,1,0:T(8,128)S(1)} %select_maximum_fusion.refs_0_.payload_in, f32[5,8,256]{2,1,0:T(8,128)S(1)} %collective-permute-done.4.refs_0_.payload_before, f32[2,256,256]{2,1,0:T(8,128)S(1)} %get-tuple-element.24.own, f32[2,256,256]{2,1,0:T(8,128)S(1)} %get-tuple-element.27.before), custom_call_target="tpu_custom_call" | custom-call | flops 1048576 | bytes 12582912 | tf_op jit(solution)/shard_map/pallas_call | solution.py:319
  23.7 5.4 %collective-permute-done.5.across_in = f32[256,256]{1,0:T(8,128)S(1)} collective-permute-done((f32[256,256]{1,0:T(8,128)S(1)}, f32[256,256]{1,0:T(8,128)S(1)}, u32[]{:S(2)}, u32[]{:S(2)}) %collective-permute-start.5) | collective-permute-done | bytes 262176 | tf_op jit(solution)/shard_map/ppermute | solution.py:318
  29.1 1.7 %shard_map.69 = f32[256,4096]{1,0:T(8,128)} custom-call(f32[256,4096]{1,0:T(8,128)} %shard_map.68.image_in, f32[256,256]{1,0:T(8,128)S(1)} %collective-permute-done.5.across_in), custom_call_target="tpu_custom_call", output_to_operand_aliasing={{}: (0, {})} | custom-call | tf_op jit(solution)/shard_map/pallas_call | solution.py:328
Async XLA Ops:
  0.0 10.4 %collective-permute-start = (f32[1,1,2,256,256]{4,3,2,1,0:T(8,128)}, f32[1,1,2,256,256]{4,3,2,1,0:T(8,128)S(1)}, u32[]{:S(2)}, u32[]{:S(2)}) collective-permute-start(f32[1,1,2,256,256]{4,3,2,1,0:T(8,128)} %refs_1_.1), channel_id=1, source_target_pairs={{0,4},{4,8},{8,12},{12,16},{16,20},{20,24},{24,28},{28,0},{1,5},{5... | collective-permute-start | bytes 1572872 | tf_op jit(solution)/shard_map/ppermute | solution.py:269
  1.8 8.6 %collective-permute-start.1 = (f32[4,256]{1,0:T(4,128)}, f32[4,256]{1,0:T(4,128)S(1)}, u32[]{:S(2)}, u32[]{:S(2)}) collective-permute-start(f32[4,256]{1,0:T(4,128)} %get-tuple-element.19), channel_id=1, source_target_pairs={{0,1},{1,2},{2,3},{3,0},{4,5},{5,6},{6,7},{7,4},{8,9},{9,10},{10,1... | collective-permute-start | bytes 12296 | tf_op jit(solution)/shard_map/ppermute | solution.py:266
  4.4 6.0 %collective-permute-start.2 = (f32[4,256]{1,0:T(4,128)}, f32[4,256]{1,0:T(4,128)S(1)}, u32[]{:S(2)}, u32[]{:S(2)}) collective-permute-start(f32[4,256]{1,0:T(4,128)} %get-tuple-element.20), channel_id=1, source_target_pairs={{0,2},{1,3},{2,0},{3,1},{4,6},{5,7},{6,4},{7,5},{8,10},{9,11},{10,... | collective-permute-start | bytes 12296 | tf_op jit(solution)/shard_map/ppermute | solution.py:266
  7.0 3.8 %collective-permute-start.3 = (f32[4,256]{1,0:T(4,128)}, f32[4,256]{1,0:T(4,128)S(1)}, u32[]{:S(2)}, u32[]{:S(2)}) collective-permute-start(f32[4,256]{1,0:T(4,128)} %get-tuple-element.21), channel_id=1, source_target_pairs={{0,3},{1,0},{2,1},{3,2},{4,7},{5,4},{6,5},{7,6},{8,11},{9,8},{10,9... | collective-permute-start | bytes 12296 | tf_op jit(solution)/shard_map/ppermute | solution.py:266
  11.5 4.4 %collective-permute-start.4 = (f32[5,8,256]{2,1,0:T(8,128)S(1)}, f32[5,8,256]{2,1,0:T(8,128)S(1)}, u32[]{:S(2)}, u32[]{:S(2)}) collective-permute-start(f32[5,8,256]{2,1,0:T(8,128)S(1)} %select_maximum_fusion.refs_0_.payload_in), channel_id=1, source_target_pairs={{0,4},{4,8},{8,12},{12,16},{16,20},{20,24},{24,28},{28,0},{1,5},{5... | collective-permute-start | bytes 122888 | tf_op jit(solution)/shard_map/ppermute | solution.py:273
  18.8 10.3 %collective-permute-start.5 = (f32[256,256]{1,0:T(8,128)S(1)}, f32[256,256]{1,0:T(8,128)S(1)}, u32[]{:S(2)}, u32[]{:S(2)}) collective-permute-start(f32[256,256]{1,0:T(8,128)S(1)} %get-tuple-element.28), channel_id=1, source_target_pairs={{0,1},{1,2},{2,3},{3,0},{4,5},{5,6},{6,7},{7,4},{8,9},{9,10},{10,1... | collective-permute-start | bytes 786440 | tf_op jit(solution)/shard_map/ppermute | solution.py:318

commit v3 on v2

v3 whole, which is shorter than its diff:
```python
import functools
import math

import jax
import jax.numpy as jnp
from jax import lax
from jax.experimental import pallas as pl
from jax.experimental.pallas import tpu as pltpu
from jax.sharding import PartitionSpec as P

TAPS = 8
STRIP = 256
BAND = 4096
SUB = 256
HALF = SUB // 2
BLOCK = 64
TILE = 16
LAST = BAND // SUB - 1
PARTS = 8


def numbers_kernel(n, tracks, counts, offsets, out):
    me = lax.axis_index("chan")
    lane = lax.broadcasted_iota(jnp.int32, (1, out.shape[1]), 1)
    block = lane // BLOCK
    lines = []
    for k in range(n):
        source = sender(n, me, k)
        target = jnp.zeros_like(lane)
        for b in range(tracks.shape[-1]):
            target = jnp.where(block == b, tracks[0, 0, source, b], target)
        lines += [target, jnp.where(block < counts[0, 0, source], 1, 0)]
    corners = jnp.zeros_like(lane)
    for place in range(4):
        corners = jnp.where(lane == place, offsets[0, 0, place // 2, place % 2], corners)
    lines += [corners] * (out.shape[0] - 2 * n)
    out[...] = jnp.concatenate(lines, axis=0).astype(jnp.float32)


def tables_kernel(numbers_in, ahead, behind, numbers):
    numbers[...] = numbers_in[...]
    shape = (SUB, SUB)
    for across, out in ((1, ahead), (0, behind)):
        j = lax.broadcasted_iota(jnp.int32, shape, across)
        x = lax.broadcasted_iota(jnp.int32, shape, 1 - across)
        turn = jnp.where(j > HALF, (j - HALF) * x + 3 * SUB // 4, j * x) & (SUB - 1)
        turn = jnp.minimum(turn, SUB - turn).astype(jnp.float32)
        half_angle = cosine(turn * (math.pi / SUB))
        high, low = halves(2.0 * half_angle * half_angle - 1.0)
        out[:SUB] = high
        out[SUB:] = low


def halves(value):
    high = value.astype(jnp.bfloat16)
    low = (value - high.astype(jnp.float32)).astype(jnp.bfloat16)
    return high, low


def cosine(angle):
    square = angle * angle
    series = jnp.float32(-1.0 / math.factorial(14))
    for order in range(12, -1, -2):
        sign = 1.0 if order % 4 == 0 else -1.0
        series = series * square + jnp.float32(sign / math.factorial(order))
    return series


def taper(offset):
    series = cosine(offset * (math.pi / TAPS))
    return jnp.where(jnp.abs(offset) < TAPS / 2, series * series, 0.0)


def folded(position, rho):
    base = jnp.floor(position) - (TAPS // 2 - 1)

    def cell_at(residue):
        ahead = residue - base
        ahead = ahead - TILE * jnp.floor(ahead * (1.0 / TILE))
        return base + ahead, ahead < TAPS

    cell, inside = cell_at(rho)
    direct = inside & (cell <= HALF)
    near = jnp.where(direct, taper(cell - position), 0.0)
    mirror, inside = cell_at(-rho)
    far = jnp.where(inside & (mirror > HALF), taper(mirror - position), 0.0)
    turn = jnp.where(direct, cell - rho, SUB - mirror - rho) * (1.0 / TILE)
    return near + far, near - far, turn.astype(jnp.bfloat16)


def sender(n, me, k):
    return me ^ k if n == 4 else lax.rem(me - k + n, n)


def exchange(n, me, visibilities, positions, numbers):
    def slot(index):
        parts = [lax.dynamic_index_in_dim(a[0, 0], index, 0, False) for a in (visibilities, positions)]
        return jnp.concatenate(parts, axis=0)

    def swap(piece, bit):
        return lax.ppermute(piece, "chan", [(i, i ^ bit) for i in range(n)])

    if n != 4:
        pieces = [slot(me)]
        for k in range(1, n):
            ring = [(i, (i + k) % n) for i in range(n)]
            pieces.append(lax.ppermute(slot(lax.rem(me + k, n)), "chan", ring))
        return pieces
    near = swap(jnp.concatenate([slot(me ^ 1), slot(me ^ 3)], axis=0), 1)
    near, numbers = lax.optimization_barrier((near, numbers))
    far = swap(jnp.concatenate([slot(me ^ 2), near[4:]], axis=0), 2)
    return [slot(me), near[:4], far]


def fill_factors(n, payload, le, lo, we, wo):
    rows = payload.shape[-1]
    rho = lax.broadcasted_iota(jnp.int32, (TILE, rows), 0).astype(jnp.float32)
    zero = jnp.zeros((TILE, rows), jnp.bfloat16)
    for k in range(n):
        piece = payload[4 * k : 4 * k + 4]
        target = payload[4 * n + 2 * k : 4 * n + 2 * k + 1]
        live = payload[4 * n + 2 * k + 1 : 4 * n + 2 * k + 2]
        real = piece[0:1] * live
        imag = piece[1:2] * live
        u_position = piece[2:3]
        u_even, u_odd, u_turn = folded(u_position, rho)
        v_even, v_odd, v_turn = folded(piece[3:4], rho)
        middle = taper(HALF - u_position)
        place = pl.ds(k * rows, rows)

        def put(ref, row, pair):
            for part, value in enumerate(pair):
                start = part * (ref.shape[0] // 2) + row
                ref[start : start + TILE, place] = value

        first = target == 0.0
        evens = [halves(jnp.where(first, u_even, 0.0)), halves(jnp.where(first, 0.0, u_even))]
        odds = [halves(jnp.where(first, u_odd, 0.0)), halves(jnp.where(first, 0.0, u_odd))]
        for turn in range(HALF // TILE):
            chosen = u_turn == turn
            for s in range(2):
                row = s * HALF + turn * TILE
                put(le, row, [jnp.where(chosen, e, zero) for e in evens[s]])
                put(lo, row, [jnp.where(chosen, o, zero) for o in odds[s]])
        middles = jnp.where(
            (rho == 0) & first, middle, jnp.where((rho == 8) & jnp.logical_not(first), middle, 0.0)
        )
        put(le, 2 * HALF, halves(middles))
        for ref, cosine, sine in (
            (we, real * v_even, imag * v_odd),
            (wo, imag * v_even, -real * v_odd),
        ):
            cosine, sine = halves(cosine), halves(sine)
            for turn in range(HALF // TILE):
                chosen = v_turn == turn
                put(ref, turn * TILE, [jnp.where(chosen, c, zero) for c in cosine])
                pair = [jnp.where(chosen, c, zero) for c in sine]
                if turn == 0:
                    top = v_turn == HALF // TILE
                    pair = [jnp.where(top, c, p) for c, p in zip(cosine, pair)]
                put(ref, HALF + turn * TILE, pair)


def product(a, b, contract):
    rows, half = a.shape[0] // 2, b.shape[0] // 2

    def dot(left, right):
        numbers = (((1,), (contract,)), ((), ()))
        return lax.dot_general(left, right, numbers, preferred_element_type=jnp.float32)

    main = dot(a, b[:half])
    return main[:rows] + main[rows:] + dot(a[:rows], b[half:])


def picture_kernel(n, scale, spilled, *refs):
    count = 5 if spilled else 4
    payload, screens_in, ahead, behind = refs[:4]
    pictures, across = refs[count : count + 2]
    corners, le, lo, we, wo, sems = refs[count + 2 : count + 8]
    copies = [pltpu.make_async_copy(payload.at[pl.ds(6 * n, 1)], corners, sems.at[0])]
    if spilled:
        screens = screens_in.at[0, 0]
    else:
        screens = refs[-1]
        for part in range(PARTS):
            place = (part * 2 // PARTS, pl.ds(part % (PARTS // 2) * (2 * SUB // PARTS), 2 * SUB // PARTS))
            copies.append(
                pltpu.make_async_copy(
                    screens_in.at[0, 0].at[place], screens.at[place], sems.at[1 + part]
                )
            )
    for copy in copies:
        copy.start()
    fill_factors(n, payload, le, lo, we, wo)
    even = product(le[...], we[...], 1)
    odd = product(lo[...], wo[...], 1)
    row_ids = lax.broadcasted_iota(jnp.int32, (SUB, SUB), 0)
    col_ids = lax.broadcasted_iota(jnp.int32, (SUB, SUB), 1)
    first_row = lax.broadcasted_iota(jnp.int32, (HALF, SUB), 0) == 0
    total = refs[4][...] if spilled else jnp.zeros((SUB, SUB), jnp.float32)
    grids = []
    for s in range(2):
        middle = even[2 * HALF + 8 * s : 2 * HALF + 8 * s + 1]
        lower = jnp.where(first_row, middle, odd[s * HALF : (s + 1) * HALF])
        grids += [even[s * HALF : (s + 1) * HALF], lower]
    half_way = product(
        jnp.concatenate(halves(jnp.concatenate(grids, axis=0)), axis=0), behind[...], 0
    )
    for s in range(2):
        image = jnp.concatenate(halves(half_way[s * SUB : (s + 1) * SUB]), axis=0)
        image = product(ahead[...], image, 0)
        if s == 0:
            copies[0].wait()
        for copy in copies[1 + s * PARTS // 2 : 1 + (s + 1) * PARTS // 2]:
            copy.wait()
        image = screens[s] * (image * scale)
        row = corners[0, 2 * s].astype(jnp.int32)
        col = corners[0, 2 * s + 1].astype(jnp.int32)
        shift = lax.rem(col, SUB)
        image = pltpu.roll(pltpu.roll(image, row, 0), shift, 1)
        here = (row_ids < row) if spilled else (row_ids >= row)
        image = jnp.where(here, image, 0.0)
        pictures[s] = image
        beyond = (col_ids < shift) & (col // SUB == LAST)
        total = total + jnp.where(beyond, image, 0.0)
    across[...] = total


def paste_kernel(n, payload_in, payload_before, own, before, out, block_out, corners, sems):
    copies = [
        pltpu.make_async_copy(source.at[pl.ds(6 * n, 1)], corners.at[pl.ds(i, 1)], sems.at[i])
        for i, source in enumerate((payload_in, payload_before))
    ]
    for copy in copies:
        copy.start()
    out[...] = jnp.zeros_like(out)
    for copy in copies:
        copy.wait()
    col_ids = lax.broadcasted_iota(jnp.int32, (SUB, SUB), 1)
    for i, pictures in enumerate((own, before)):
        for s in range(2):
            col = corners[i, 2 * s + 1].astype(jnp.int32)
            shift = lax.rem(col, SUB)
            block = col // SUB
            image = pictures[s]
            place = pl.ds(pl.multiple_of(block * SUB, SUB), SUB)
            out[:, place] += jnp.where(col_ids >= shift, image, 0.0)

            @pl.when(block < LAST)
            def _():
                place = pl.ds(pl.multiple_of((block + 1) * SUB, SUB), SUB)
                out[:, place] += jnp.where(col_ids < shift, image, 0.0)

    block_out[...] = out[:, :SUB]


def finish_kernel(image_in, block, across, image_out, total, sem):
    total[...] = block[...] + across[...]
    copy = pltpu.make_async_copy(total, image_out.at[:, pl.ds(0, SUB)], sem)
    copy.start()
    copy.wait()


def shards(mesh, visibilities, positions, tracks, counts, screens, offsets):
    n = mesh.shape["chan"]
    facets = mesh.shape["facet"]
    rows = visibilities.shape[-1]
    vmem = pl.BlockSpec(memory_space=pltpu.VMEM)
    anywhere = pl.BlockSpec(memory_space=pl.ANY)
    hbm = pl.BlockSpec(memory_space=pltpu.HBM)
    facet_ring = [(i, (i + 1) % facets) for i in range(facets)]

    numbers = pl.pallas_call(
        functools.partial(numbers_kernel, n),
        out_shape=jax.ShapeDtypeStruct((2 * n + 8, rows), jnp.float32),
        in_specs=[pl.BlockSpec(memory_space=pltpu.SMEM)] * 3,
        out_specs=vmem,
        compiler_params=pltpu.CompilerParams(vmem_limit_bytes=56 << 20),
    )(tracks, counts, offsets)
    pieces = exchange(n, lax.axis_index("chan"), visibilities, positions, numbers)
    screens_before = lax.ppermute(screens, "facet", facet_ring)
    ahead, behind, numbers = pl.pallas_call(
        tables_kernel,
        out_shape=(
            jax.ShapeDtypeStruct((2 * SUB, SUB), jnp.bfloat16),
            jax.ShapeDtypeStruct((2 * SUB, SUB), jnp.bfloat16),
            jax.ShapeDtypeStruct((2 * n + 8, rows), jnp.float32),
        ),
        in_specs=[vmem],
        out_specs=(vmem, vmem, vmem),
        compiler_params=pltpu.CompilerParams(vmem_limit_bytes=8 << 20),
        cost_estimate=pl.CostEstimate(flops=4 << 20, bytes_accessed=1 << 20, transcendentals=0),
    )(numbers)
    pieces[0], screens_before = lax.optimization_barrier((pieces[0], screens_before))
    payload = jnp.concatenate(pieces + [numbers], axis=0)
    payload_before = lax.ppermute(payload, "facet", facet_ring)

    depth = n * rows
    picture = jax.ShapeDtypeStruct((SUB, SUB), jnp.float32)
    scale = 1.0 / (2.0 * math.sqrt(n * rows))
    factor_rows = 2 * (4 * HALF + TILE + 2 * SUB)
    room = 24 + (2 * factor_rows * depth >> 20)

    def pictures_of(spilled, *operands):
        return pl.pallas_call(
            functools.partial(picture_kernel, n, scale, spilled),
            out_shape=(jax.ShapeDtypeStruct((2, SUB, SUB), jnp.float32), picture),
            in_specs=[vmem, vmem if spilled else anywhere, vmem, vmem]
            + [vmem] * (len(operands) - 4),
            out_specs=(vmem, vmem),
            scratch_shapes=[
                pltpu.SMEM((1, rows), jnp.float32),
                pltpu.VMEM((4 * HALF + 2 * TILE, depth), jnp.bfloat16),
                pltpu.VMEM((4 * HALF, depth), jnp.bfloat16),
                pltpu.VMEM((2 * SUB, depth), jnp.bfloat16),
                pltpu.VMEM((2 * SUB, depth), jnp.bfloat16),
                pltpu.SemaphoreType.DMA((1 + PARTS,)),
            ]
            + [pltpu.VMEM((2, SUB, SUB), jnp.float32)] * (not spilled),
            compiler_params=pltpu.CompilerParams(vmem_limit_bytes=max(room << 20, 0 if spilled else 209 << 18)),
            cost_estimate=pl.CostEstimate(
                flops=2 * depth * SUB * SUB * 4, bytes_accessed=4 << 20, transcendentals=0
            ),
        )(*operands)

    own, across = pictures_of(False, payload, screens, ahead, behind)
    before, across = pictures_of(True, payload_before, screens_before, ahead, behind, across)
    across = lax.ppermute(across, "chan", [(i, (i + 1) % n) for i in range(n)])
    image, block = pl.pallas_call(
        functools.partial(paste_kernel, n),
        out_shape=(jax.ShapeDtypeStruct((STRIP, BAND), jnp.float32), picture),
        in_specs=[anywhere] * 2 + [vmem] * 2,
        out_specs=(vmem, vmem),
        scratch_shapes=[pltpu.SMEM((2, rows), jnp.float32), pltpu.SemaphoreType.DMA((2,))],
        compiler_params=pltpu.CompilerParams(vmem_limit_bytes=16 << 20),
        cost_estimate=pl.CostEstimate(flops=1 << 20, bytes_accessed=12 << 20, transcendentals=0),
    )(payload, payload_before, own, before)
    return pl.pallas_call(
        finish_kernel,
        out_shape=jax.ShapeDtypeStruct((STRIP, BAND), jnp.float32),
        in_specs=[anywhere, vmem, vmem],
        out_specs=anywhere,
        scratch_shapes=[pltpu.VMEM((STRIP, SUB), jnp.float32), pltpu.SemaphoreType.DMA],
        input_output_aliases={0: 0},
        compiler_params=pltpu.CompilerParams(vmem_limit_bytes=4 << 20),
    )(image, block, across)


def solution(mesh):
    return jax.shard_map(
        functools.partial(shards, mesh),
        mesh=mesh,
        in_specs=(
            P("facet", "chan", None, None, None),
            P("facet", "chan", None, None, None),
            P("facet", "chan", None, None),
            P("facet", "chan", None),
            P("facet", "chan", None, None, None),
            P("facet", "chan", None, None),
        ),
        out_specs=P("facet", "chan"),
        check_vma=False,
    )
```

time: 31 us -> 28.5 us (0.919)
  Pallas kernels: 12.2 us -> 10.4 us
  local copies, waits for them, and re-layouts: 0 us -> 1.52 us
  waiting for transfers between devices: 8.71 us -> 7.44 us
  other arithmetic: 0.71 us -> 0.04 us
  starting transfers between devices: 9.14 us -> 8.72 us
    ppermute x1, waiting for transfers between devices: 1.6 us -> 0.54 us  [shards(): screens_before = lax.ppermute(screens, 'facet', facet_ring)]
    pallas_call x1, Pallas kernels: 1.71 us -> 0.74 us  [shards(): pl.pallas_call(finish_kernel, out_shape=jax.ShapeDtypeStruct((STRIP, BAND...]
    pallas_call x2, Pallas kernels: 5.84 us -> 5.03 us  [pictures_of(): pl.pallas_call(functools.partial(picture_kernel, n, scale, spilled), out_...]
    squeeze x0 -> x1, local copies, waits for them, and re-layouts: none -> 0.8 us  [slot(): lax.dynamic_index_in_dim(a[0, 0], index, 0, False)]
    ppermute x3 -> x2, starting transfers between devices: 6.51 us -> 5.74 us  [swap(): return lax.ppermute(piece, 'chan', [(i, i ^ bit) for i in range(n)])]
    unnamed x0 -> x2, local copies, waits for them, and re-layouts: none -> 0.72 us
    concatenate x1 -> x4, other arithmetic: 0.71 us -> 0.04 us  [the longest x1 0.01 us: exchange(): far = swap(jnp.concatenate([slot(me ^ 2), near[4:]], axis=0), 2)]
    ppermute x1, waiting for transfers between devices: 5.43 us -> 5.02 us  [shards(): across = lax.ppermute(across, 'chan', [(i, (i + 1) % n) for i in range(n)])]
  transfers between devices with their start and end apart: 6 -> 5, of which waited for: 4 -> 4; matrix products, arithmetic and copies ran while one was open for 0% -> 3% of each run, Pallas kernels for 25% -> 26%
where the time goes in v3:
time: 28.5 us; the launch traced here: 28.2 us
  Pallas kernels  10.4 us (36%)
  starting transfers between devices  8.72 us (31%)
  waiting for transfers between devices  7.44 us (26%)
  local copies, waits for them, and re-layouts  1.52 us (5%)
    ppermute x2, starting transfers between devices, swap(): return lax.ppermute(piece, 'chan', [(i, i ^ bit) for i in range(n)])  5.74 us
    pallas_call x2, Pallas kernels, pictures_of(): pl.pallas_call(functools.partial(picture_kernel, n, scale, spilled), out_...  5.03 us
    ppermute x1, waiting for transfers between devices, shards(): across = lax.ppermute(across, 'chan', [(i, (i + 1) % n) for i in range(n)])  5.02 us
    pallas_call x1, Pallas kernels, shards(): pl.pallas_call(functools.partial(paste_kernel, n), out_shape=(jax.ShapeDt...  2.83 us
    ppermute x1, starting transfers between devices, shards(): across = lax.ppermute(across, 'chan', [(i, (i + 1) % n) for i in range(n)])  2.39 us
    ppermute x1, waiting for transfers between devices, shards(): payload_before = lax.ppermute(payload, 'facet', facet_ring)  1.6 us
    pallas_call x1, Pallas kernels, shards(): pl.pallas_call(functools.partial(numbers_kernel, n), out_shape=jax.ShapeD...  1.36 us
    squeeze x1, local copies, waits for them, and re-layouts, slot(): lax.dynamic_index_in_dim(a[0, 0], index, 0, False)  0.8 us
  transfers between devices with their start and end apart: 5, of which 4 were waited for; matrix products, arithmetic and copies ran while one was open for 3% of the time, Pallas kernels for 26%

profile of v3, /device:TPU:0, one launch (start us, length us, event | category | flops | bytes accessed | tf_op | source)
XLA Modules:
  0.0 28.2 jit_solution(3375622063536310134)
XLA Ops:
  0.0 0.5 %collective-permute-start = (f32[1,1,2,256,256]{4,3,2,1,0:T(8,128)}, f32[1,1,2,256,256]{4,3,2,1,0:T(8,128)S(1)}, u32[]{:S(2)}, u32[]{:S(2)}) collective-permute-start(f32[1,1,2,256,256]{4,3,2,1,0:T(8,128)} %refs_1_.1), channel_id=1, source_target_pairs={{0,4},{4,8},{8,12},{12,16},{16,20},{20,24},{24,28},{28,0},{1,5},{5... | collective-permute-start | bytes 1572872 | tf_op jit(solution)/shard_map/ppermute | solution.py:281
  0.5 0.8 %dynamic-slice_bitcast_fusion.6 = (f32[2,256]{1,0:T(2,128)S(1)}, f32[2,256]{1,0:T(2,128)S(1)}, f32[2,256]{1,0:T(2,128)S(1)}, f32[2,256]{1,0:T(2,128)S(1)}, f32[2...) fusion(f32[1,1,4,2,256]{4,3,2,1,0:T(2,128)} %param.7, s32[]{:T(128)S(6)} %select_n.17, ...), kind=kLoop, calls=%fused_computation.10 | loop fusion | bytes 32784 | tf_op jit(solution)/shard_map/jit(dynamic_index_in_dim)/squeeze | solution.py:97
  1.3 2.6 %collective-permute-start.1 = (f32[8,256]{1,0:T(8,128)S(1)}, f32[8,256]{1,0:T(8,128)S(1)}, u32[]{:S(2)}, u32[]{:S(2)}) collective-permute-start(f32[8,256]{1,0:T(8,128)S(1)} %pad_maximum_fusion.1), channel_id=1, source_target_pairs={{0,1},{1,0},{2,3},{3,2},{4,5},{5,4},{6,7},{7,6},{8,9},{9,8},{10,11... | collective-permute-start | bytes 24584 | tf_op jit(solution)/shard_map/ppermute | solution.py:101
  3.9 1.4 %shard_map.64.numbers_in = f32[16,256]{1,0:T(8,128)} custom-call(s32[1,1,4,4]{3,2,1,0:T(4,128)} %tracks.1, s32[1,1,4]{2,1,0:T(1,128)} %counts.1, s32[1,1,2,2]{3,2,1,0:T(2,128)} %offsets.1), custom_call_target="tpu_custom_call" | custom-call | tf_op jit(solution)/shard_map/pallas_call | solution.py:273
  5.3 0.3 collective-permute-done.1
  5.6 3.1 %collective-permute-start.2 = (f32[8,256]{1,0:T(8,128)S(1)}, f32[8,256]{1,0:T(8,128)S(1)}, u32[]{:S(2)}, u32[]{:S(2)}) collective-permute-start(f32[8,256]{1,0:T(8,128)S(1)} %pad_maximum_fusion.2), channel_id=1, source_target_pairs={{0,2},{1,3},{2,0},{3,1},{4,6},{5,7},{6,4},{7,5},{8,10},{9,11},{10,... | collective-permute-start | bytes 24584 | tf_op jit(solution)/shard_map/ppermute | solution.py:101
  8.7 0.0 copy-start
  8.7 0.7 %copy-done = f32[16,256]{1,0:T(8,128)S(1)} copy-done((f32[16,256]{1,0:T(8,128)S(1)}, f32[16,256]{1,0:T(8,128)}, u32[]{:S(2)}) %copy-start) | copy-done | bytes 16408
  9.4 0.5 %shard_map.65 = (bf16[512,256]{1,0:T(8,128)(2,1)S(1)}, bf16[512,256]{1,0:T(8,128)(2,1)S(1)}, f32[16,256]{1,0:T(8,128)S(1)}) custom-call(f32[16,256]{1,0:T(8,128)S(1)} %copy-done), custom_call_target="tpu_custom_call" | custom-call | flops 4194304 | bytes 1048576 | tf_op jit(solution)/shard_map/pallas_call | solution.py:282
  9.9 0.5 %collective-permute-done.refs_1_ = f32[1,1,2,256,256]{4,3,2,1,0:T(8,128)S(1)} collective-permute-done((f32[1,1,2,256,256]{4,3,2,1,0:T(8,128)}, f32[1,1,2,256,256]{4,3,2,1,0:T(8,128)S(1)}, u32[]{:S(2)}, u32[]{:S(2)}) %collective-permute-start) | collective-permute-done | bytes 524320 | tf_op jit(solution)/shard_map/ppermute | solution.py:281
  10.4 0.0 collective-permute-done.2
  10.4 0.1 collective-permute-start.3
  10.6 2.5 %shard_map.66 = (f32[2,256,256]{2,1,0:T(8,128)S(1)}, f32[256,256]{1,0:T(8,128)S(1)}) custom-call(f32[32,256]{1,0:T(8,128)S(1)} %pad_maximum_fusion.refs_0_.payload_in, f32[1,1,2,256,256]{4,3,2,1,0:T(8,128)} %refs_1_.1, bf16[512,256]{1,0:T(8,128)(2,1)S(1)} %get-tuple-element.20.refs_2_, bf16[512,256]{1,0:T(8,128)(2,1)S(1)} %get-tuple-element.21.refs_3_), custom_call_target="tpu_custom_call" | custom-call | flops 536870912 | bytes 4194304 | tf_op jit(solution)/shard_map/pallas_call | solution.py:305
  13.1 1.6 %collective-permute-done.3.refs_0_.payload_before = f32[32,256]{1,0:T(8,128)S(1)} collective-permute-done((f32[32,256]{1,0:T(8,128)S(1)}, f32[32,256]{1,0:T(8,128)S(1)}, u32[]{:S(2)}, u32[]{:S(2)}) %collective-permute-start.3) | collective-permute-done | bytes 32800 | tf_op jit(solution)/shard_map/ppermute | solution.py:296
  14.7 2.5 %shard_map.67 = (f32[2,256,256]{2,1,0:T(8,128)S(1)}, f32[256,256]{1,0:T(8,128)S(1)}) custom-call(f32[32,256]{1,0:T(8,128)S(1)} %collective-permute-done.3.refs_0_.payload_before, f32[1,1,2,256,256]{4,3,2,1,0:T(8,128)S(1)} %collective-permute-done.refs_1_, bf16[512,256]{1,0:T(8,128)(2,1)S(1)} %get-tuple-element.20.refs_2_, ...), custom_call_target="tpu_custom_call" | custom-call | flops 536870912 | bytes 4194304 | tf_op jit(solution)/shard_map/pallas_call | solution.py:305
  17.2 2.4 %collective-permute-start.4 = (f32[256,256]{1,0:T(8,128)S(1)}, f32[256,256]{1,0:T(8,128)S(1)}, u32[]{:S(2)}, u32[]{:S(2)}) collective-permute-start(f32[256,256]{1,0:T(8,128)S(1)} %get-tuple-element.28), channel_id=1, source_target_pairs={{0,1},{1,2},{2,3},{3,0},{4,5},{5,6},{6,7},{7,4},{8,9},{9,10},{10,1... | collective-permute-start | bytes 786440 | tf_op jit(solution)/shard_map/ppermute | solution.py:328
  19.6 2.8 %shard_map.68 = (f32[256,4096]{1,0:T(8,128)}, f32[256,256]{1,0:T(8,128)S(1)}) custom-call(f32[32,256]{1,0:T(8,128)S(1)} %pad_maximum_fusion.refs_0_.payload_in, f32[32,256]{1,0:T(8,128)S(1)} %collective-permute-done.3.refs_0_.payload_before, f32[2,256,256]{2,1,0:T(8,128)S(1)} %get-tuple-element.22.own, f32[2,256,256]{2,1,0:T(8,128)S(1)} %get-tuple-element.25.before), custom_call_target="tpu_custom_call" | custom-call | flops 1048576 | bytes 12582912 | tf_op jit(solution)/shard_map/pallas_call | solution.py:329
  22.4 5.0 %collective-permute-done.4.across = f32[256,256]{1,0:T(8,128)S(1)} collective-permute-done((f32[256,256]{1,0:T(8,128)S(1)}, f32[256,256]{1,0:T(8,128)S(1)}, u32[]{:S(2)}, u32[]{:S(2)}) %collective-permute-start.4) | collective-permute-done | bytes 262176 | tf_op jit(solution)/shard_map/ppermute | solution.py:328
  27.5 0.7 %shard_map.69 = f32[256,4096]{1,0:T(8,128)} custom-call(f32[256,4096]{1,0:T(8,128)} %get-tuple-element.26.image_in, f32[256,256]{1,0:T(8,128)S(1)} %get-tuple-element.27.block, f32[256,256]{1,0:T(8,128)S(1)} %collective-permute-done.4.across), custom_call_target="tpu_custom_call", output_to_operand_aliasing={{}: (0, {})} | custom-call | tf_op jit(solution)/shard_map/pallas_call | solution.py:338
  (5 shorter events, 0.0 us)
Async XLA Ops:
  0.0 10.4 %collective-permute-start = (f32[1,1,2,256,256]{4,3,2,1,0:T(8,128)}, f32[1,1,2,256,256]{4,3,2,1,0:T(8,128)S(1)}, u32[]{:S(2)}, u32[]{:S(2)}) collective-permute-start(f32[1,1,2,256,256]{4,3,2,1,0:T(8,128)} %refs_1_.1), channel_id=1, source_target_pairs={{0,4},{4,8},{8,12},{12,16},{16,20},{20,24},{24,28},{28,0},{1,5},{5... | collective-permute-start | bytes 1572872 | tf_op jit(solution)/shard_map/ppermute | solution.py:281
  1.3 4.3 %collective-permute-start.1 = (f32[8,256]{1,0:T(8,128)S(1)}, f32[8,256]{1,0:T(8,128)S(1)}, u32[]{:S(2)}, u32[]{:S(2)}) collective-permute-start(f32[8,256]{1,0:T(8,128)S(1)} %pad_maximum_fusion.1), channel_id=1, source_target_pairs={{0,1},{1,0},{2,3},{3,2},{4,5},{5,4},{6,7},{7,6},{8,9},{9,8},{10,11... | collective-permute-start | bytes 24584 | tf_op jit(solution)/shard_map/ppermute | solution.py:101
  5.6 4.9 %collective-permute-start.2 = (f32[8,256]{1,0:T(8,128)S(1)}, f32[8,256]{1,0:T(8,128)S(1)}, u32[]{:S(2)}, u32[]{:S(2)}) collective-permute-start(f32[8,256]{1,0:T(8,128)S(1)} %pad_maximum_fusion.2), channel_id=1, source_target_pairs={{0,2},{1,3},{2,0},{3,1},{4,6},{5,7},{6,4},{7,5},{8,10},{9,11},{10,... | collective-permute-start | bytes 24584 | tf_op jit(solution)/shard_map/ppermute | solution.py:101
  8.7 0.7 %copy-start = (f32[16,256]{1,0:T(8,128)S(1)}, f32[16,256]{1,0:T(8,128)}, u32[]{:S(2)}) copy-start(f32[16,256]{1,0:T(8,128)} %shard_map.64.numbers_in) | copy-start | bytes 49156
  10.4 4.3 %collective-permute-start.3 = (f32[32,256]{1,0:T(8,128)S(1)}, f32[32,256]{1,0:T(8,128)S(1)}, u32[]{:S(2)}, u32[]{:S(2)}) collective-permute-start(f32[32,256]{1,0:T(8,128)S(1)} %pad_maximum_fusion.refs_0_.payload_in), channel_id=1, source_target_pairs={{0,4},{4,8},{8,12},{12,16},{16,20},{20,24},{24,28},{28,0},{1,5},{5... | collective-permute-start | bytes 98312 | tf_op jit(solution)/shard_map/ppermute | solution.py:296
  17.2 10.2 %collective-permute-start.4 = (f32[256,256]{1,0:T(8,128)S(1)}, f32[256,256]{1,0:T(8,128)S(1)}, u32[]{:S(2)}, u32[]{:S(2)}) collective-permute-start(f32[256,256]{1,0:T(8,128)S(1)} %get-tuple-element.28), channel_id=1, source_target_pairs={{0,1},{1,2},{2,3},{3,0},{4,5},{5,6},{6,7},{7,4},{8,9},{9,10},{10,1... | collective-permute-start | bytes 786440 | tf_op jit(solution)/shard_map/ppermute | solution.py:328

commit v4 on v3

--- a/solution.py
+++ b/solution.py
@@ -89,7 +89,7 @@
 
 
 def sender(n, me, k):
-    return me ^ k if n == 4 else lax.rem(me - k + n, n)
+    return me ^ (0, 2, 1, 3)[k] if n == 4 else lax.rem(me - k + n, n)
 
 
 def exchange(n, me, visibilities, positions, numbers):
@@ -106,10 +106,10 @@
             ring = [(i, (i + k) % n) for i in range(n)]
             pieces.append(lax.ppermute(slot(lax.rem(me + k, n)), "chan", ring))
         return pieces
-    near = swap(jnp.concatenate([slot(me ^ 1), slot(me ^ 3)], axis=0), 1)
-    near, numbers = lax.optimization_barrier((near, numbers))
-    far = swap(jnp.concatenate([slot(me ^ 2), near[4:]], axis=0), 2)
-    return [slot(me), near[:4], far]
+    far = swap(jnp.concatenate([slot(me ^ 2), slot(me ^ 3)], axis=0), 2)
+    far, numbers = lax.optimization_barrier((far, numbers))
+    near = swap(jnp.concatenate([slot(me ^ 1), far[4:]], axis=0), 1)
+    return [slot(me), far[:4], near]
 
 
 def fill_factors(n, payload, le, lo, we, wo):
@@ -172,8 +172,23 @@
     return main[:rows] + main[rows:] + dot(a[:rows], b[half:])
 
 
-def picture_kernel(n, scale, spilled, *refs):
-    count = 5 if spilled else 4
+def picture_kernel(n, scale, turn, *refs):
+    if turn < 2:
+
+        @pl.when(lax.rem(lax.axis_index("facet"), 2) == 1 - turn)
+        def _():
+            make_pictures(n, scale, False, *refs)
+
+    else:
+        make_pictures(n, scale, True, *refs)
+
+
+def own_part(first, second):
+    return jnp.where(lax.rem(lax.axis_index("facet"), 2) == 1, first, second)
+
+
+def make_pictures(n, scale, spilled, *refs):
+    count = 6 if spilled else 4
     payload, screens_in, ahead, behind = refs[:4]
     pictures, across = refs[count : count + 2]
     corners, le, lo, we, wo, sems = refs[count + 2 : count + 8]
@@ -197,7 +212,7 @@
     row_ids = lax.broadcasted_iota(jnp.int32, (SUB, SUB), 0)
     col_ids = lax.broadcasted_iota(jnp.int32, (SUB, SUB), 1)
     first_row = lax.broadcasted_iota(jnp.int32, (HALF, SUB), 0) == 0
-    total = refs[4][...] if spilled else jnp.zeros((SUB, SUB), jnp.float32)
+    total = own_part(refs[4][...], refs[5][...]) if spilled else jnp.zeros((SUB, SUB), jnp.float32)
     grids = []
     for s in range(2):
         middle = even[2 * HALF + 8 * s : 2 * HALF + 8 * s + 1]
@@ -226,7 +241,7 @@
     across[...] = total
 
 
-def paste_kernel(n, payload_in, payload_before, own, before, out, block_out, corners, sems):
+def paste_kernel(n, payload_in, payload_before, own, own_later, before, out, block_out, corners, sems):
     copies = [
         pltpu.make_async_copy(source.at[pl.ds(6 * n, 1)], corners.at[pl.ds(i, 1)], sems.at[i])
         for i, source in enumerate((payload_in, payload_before))
@@ -242,7 +257,7 @@
             col = corners[i, 2 * s + 1].astype(jnp.int32)
             shift = lax.rem(col, SUB)
             block = col // SUB
-            image = pictures[s]
+            image = pictures[s] if i else own_part(own[s], own_later[s])
             place = pl.ds(pl.multiple_of(block * SUB, SUB), SUB)
             out[:, place] += jnp.where(col_ids >= shift, image, 0.0)
 
@@ -291,9 +306,7 @@
         compiler_params=pltpu.CompilerParams(vmem_limit_bytes=8 << 20),
         cost_estimate=pl.CostEstimate(flops=4 << 20, bytes_accessed=1 << 20, transcendentals=0),
     )(numbers)
-    pieces[0], screens_before = lax.optimization_barrier((pieces[0], screens_before))
     payload = jnp.concatenate(pieces + [numbers], axis=0)
-    payload_before = lax.ppermute(payload, "facet", facet_ring)
 
     depth = n * rows
     picture = jax.ShapeDtypeStruct((SUB, SUB), jnp.float32)
@@ -301,9 +314,10 @@
     factor_rows = 2 * (4 * HALF + TILE + 2 * SUB)
     room = 24 + (2 * factor_rows * depth >> 20)
 
-    def pictures_of(spilled, *operands):
+    def pictures_of(turn, *operands):
+        spilled = turn == 2
         return pl.pallas_call(
-            functools.partial(picture_kernel, n, scale, spilled),
+            functools.partial(picture_kernel, n, scale, turn),
             out_shape=(jax.ShapeDtypeStruct((2, SUB, SUB), jnp.float32), picture),
             in_specs=[vmem, vmem if spilled else anywhere, vmem, vmem]
             + [vmem] * (len(operands) - 4),
@@ -323,18 +337,23 @@
             ),
         )(*operands)
 
-    own, across = pictures_of(False, payload, screens, ahead, behind)
-    before, across = pictures_of(True, payload_before, screens_before, ahead, behind, across)
+    own, across = pictures_of(0, payload, screens, ahead, behind)
+    payload, across = lax.optimization_barrier((payload, across))
+    payload_before = lax.ppermute(payload, "facet", facet_ring)
+    own_later, across_later = pictures_of(1, payload, screens, ahead, behind)
+    before, across = pictures_of(
+        2, payload_before, screens_before, ahead, behind, across, across_later
+    )
     across = lax.ppermute(across, "chan", [(i, (i + 1) % n) for i in range(n)])
     image, block = pl.pallas_call(
         functools.partial(paste_kernel, n),
         out_shape=(jax.ShapeDtypeStruct((STRIP, BAND), jnp.float32), picture),
-        in_specs=[anywhere] * 2 + [vmem] * 2,
+        in_specs=[anywhere] * 2 + [vmem] * 3,
         out_specs=(vmem, vmem),
         scratch_shapes=[pltpu.SMEM((2, rows), jnp.float32), pltpu.SemaphoreType.DMA((2,))],
         compiler_params=pltpu.CompilerParams(vmem_limit_bytes=16 << 20),
         cost_estimate=pl.CostEstimate(flops=1 << 20, bytes_accessed=12 << 20, transcendentals=0),
-    )(payload, payload_before, own, before)
+    )(payload, payload_before, own, own_later, before)
     return pl.pallas_call(
         finish_kernel,
         out_shape=jax.ShapeDtypeStruct((STRIP, BAND), jnp.float32),

time: 28.5 us -> 28 us (0.982)
  waiting for transfers between devices: 7.44 us -> 5.1 us
  starting transfers between devices: 8.72 us -> 10.4 us
    ppermute x1, starting transfers between devices: 0.15 us -> 2.73 us  [shards(): payload_before = lax.ppermute(payload, 'facet', facet_ring)]
    ppermute x1, waiting for transfers between devices: 1.6 us -> 0.07 us  [shards(): payload_before = lax.ppermute(payload, 'facet', facet_ring)]
    ppermute x1, waiting for transfers between devices: 5.02 us -> 4.22 us  [shards(): across = lax.ppermute(across, 'chan', [(i, (i + 1) % n) for i in range(n)])]
    ppermute x1, starting transfers between devices: 2.39 us -> 1.63 us  [shards(): across = lax.ppermute(across, 'chan', [(i, (i + 1) % n) for i in range(n)])]
    ppermute x1, waiting for transfers between devices: 0.54 us -> 0.01 us  [shards(): screens_before = lax.ppermute(screens, 'facet', facet_ring)]
    ppermute x2, waiting for transfers between devices: 0.28 us -> 0.81 us  [swap(): return lax.ppermute(piece, 'chan', [(i, i ^ bit) for i in range(n)])]
    pallas_call x2 -> x3, Pallas kernels: 5.03 us -> 5.14 us  [pictures_of(): pl.pallas_call(functools.partial(picture_kernel, n, scale, turn), out_sha...]
where the time goes in v4:
time: 28 us; the launch traced here: 27.7 us
  Pallas kernels  10.6 us (38%)
  starting transfers between devices  10.4 us (37%)
  waiting for transfers between devices  5.1 us (18%)
  local copies, waits for them, and re-layouts  1.54 us (6%)
    ppermute x2, starting transfers between devices, swap(): return lax.ppermute(piece, 'chan', [(i, i ^ bit) for i in range(n)])  5.62 us
    pallas_call x3, Pallas kernels, pictures_of(): pl.pallas_call(functools.partial(picture_kernel, n, scale, turn), out_sha...  5.14 us
    ppermute x1, waiting for transfers between devices, shards(): across = lax.ppermute(across, 'chan', [(i, (i + 1) % n) for i in range(n)])  4.22 us
    pallas_call x1, Pallas kernels, shards(): pl.pallas_call(functools.partial(paste_kernel, n), out_shape=(jax.ShapeDt...  2.87 us
    ppermute x1, starting transfers between devices, shards(): payload_before = lax.ppermute(payload, 'facet', facet_ring)  2.73 us
    ppermute x1, starting transfers between devices, shards(): across = lax.ppermute(across, 'chan', [(i, (i + 1) % n) for i in range(n)])  1.63 us
    pallas_call x1, Pallas kernels, shards(): pl.pallas_call(functools.partial(numbers_kernel, n), out_shape=jax.ShapeD...  1.36 us
    ppermute x2, waiting for transfers between devices, swap(): return lax.ppermute(piece, 'chan', [(i, i ^ bit) for i in range(n)])  0.81 us
  transfers between devices with their start and end apart: 5, of which 4 were waited for; matrix products, arithmetic and copies ran while one was open for 3% of the time, Pallas kernels for 26%

profile of v4, /device:TPU:0, one launch (start us, length us, event | category | flops | bytes accessed | tf_op | source)
XLA Modules:
  0.0 27.7 jit_solution(10601383582534180707)
XLA Ops:
  0.0 0.5 %collective-permute-start.3 = (f32[1,1,2,256,256]{4,3,2,1,0:T(8,128)}, f32[1,1,2,256,256]{4,3,2,1,0:T(8,128)S(1)}, u32[]{:S(2)}, u32[]{:S(2)}) collective-permute-start(f32[1,1,2,256,256]{4,3,2,1,0:T(8,128)} %refs_1_.3), channel_id=1, source_target_pairs={{0,4},{4,8},{8,12},{12,16},{16,20},{20,24},{24,28},{28,0},{1,5},{5... | collective-permute-start | bytes 1572872 | tf_op jit(solution)/shard_map/ppermute | solution.py:296
  0.5 0.8 %dynamic-slice_bitcast_fusion = (f32[2,256]{1,0:T(2,128)S(1)}, f32[2,256]{1,0:T(2,128)S(1)}, f32[2,256]{1,0:T(2,128)S(1)}, f32[2,256]{1,0:T(2,128)S(1)}, f32[2,2...) fusion(f32[1,1,4,2,256]{4,3,2,1,0:T(2,128)} %param.7, s32[]{:T(128)S(6)} %select_n.20, ...), kind=kLoop, calls=%fused_computation.2 | loop fusion | bytes 32784 | tf_op jit(solution)/shard_map/jit(dynamic_index_in_dim)/squeeze | solution.py:97
  1.3 3.7 %collective-permute-start = (f32[8,256]{1,0:T(8,128)S(1)}, f32[8,256]{1,0:T(8,128)S(1)}, u32[]{:S(2)}, u32[]{:S(2)}) collective-permute-start(f32[8,256]{1,0:T(8,128)S(1)} %pad_maximum_fusion), channel_id=1, source_target_pairs={{0,2},{1,3},{2,0},{3,1},{4,6},{5,7},{6,4},{7,5},{8,10},{9,11},{10,... | collective-permute-start | bytes 24584 | tf_op jit(solution)/shard_map/ppermute | solution.py:101
  4.9 1.4 %shard_map.64.numbers_in = f32[16,256]{1,0:T(8,128)} custom-call(s32[1,1,4,4]{3,2,1,0:T(4,128)} %tracks.1, s32[1,1,4]{2,1,0:T(1,128)} %counts.1, s32[1,1,2,2]{3,2,1,0:T(2,128)} %offsets.1), custom_call_target="tpu_custom_call" | custom-call | tf_op jit(solution)/shard_map/pallas_call | solution.py:288
  6.3 0.3 collective-permute-done
  6.6 2.0 %collective-permute-start.1 = (f32[8,256]{1,0:T(8,128)S(1)}, f32[8,256]{1,0:T(8,128)S(1)}, u32[]{:S(2)}, u32[]{:S(2)}) collective-permute-start(f32[8,256]{1,0:T(8,128)S(1)} %pad_maximum_fusion.1), channel_id=1, source_target_pairs={{0,1},{1,0},{2,3},{3,2},{4,5},{5,4},{6,7},{7,6},{8,9},{9,8},{10,11... | collective-permute-start | bytes 24584 | tf_op jit(solution)/shard_map/ppermute | solution.py:101
  8.5 0.0 copy-start
  8.5 0.7 %copy-done = f32[16,256]{1,0:T(8,128)S(1)} copy-done((f32[16,256]{1,0:T(8,128)S(1)}, f32[16,256]{1,0:T(8,128)}, u32[]{:S(2)}) %copy-start) | copy-done | bytes 16408
  9.3 0.5 %shard_map.65 = (bf16[512,256]{1,0:T(8,128)(2,1)S(1)}, bf16[512,256]{1,0:T(8,128)(2,1)S(1)}, f32[16,256]{1,0:T(8,128)S(1)}) custom-call(f32[16,256]{1,0:T(8,128)S(1)} %copy-done), custom_call_target="tpu_custom_call" | custom-call | flops 4194304 | bytes 1048576 | tf_op jit(solution)/shard_map/pallas_call | solution.py:297
  9.7 0.5 %collective-permute-done.1 = f32[8,256]{1,0:T(8,128)S(1)} collective-permute-done((f32[8,256]{1,0:T(8,128)S(1)}, f32[8,256]{1,0:T(8,128)S(1)}, u32[]{:S(2)}, u32[]{:S(2)}) %collective-permute-start.1) | collective-permute-done | bytes 8224 | tf_op jit(solution)/shard_map/ppermute | solution.py:101
  10.3 0.1 shard_map.66
  10.4 2.7 %collective-permute-start.2 = (f32[32,256]{1,0:T(8,128)S(1)}, f32[32,256]{1,0:T(8,128)S(1)}, u32[]{:S(2)}, u32[]{:S(2)}) collective-permute-start(f32[32,256]{1,0:T(8,128)S(1)} %concatenate.11.refs_0_.payload_in), channel_id=1, source_target_pairs={{0,4},{4,8},{8,12},{12,16},{16,20},{20,24},{24,28},{28,0},{1,5},{5... | collective-permute-start | bytes 98312 | tf_op jit(solution)/shard_map/ppermute | solution.py:342
  13.1 2.5 %shard_map.67 = (f32[2,256,256]{2,1,0:T(8,128)S(1)}, f32[256,256]{1,0:T(8,128)S(1)}) custom-call(f32[32,256]{1,0:T(8,128)S(1)} %concatenate.11.refs_0_.payload_in, f32[1,1,2,256,256]{4,3,2,1,0:T(8,128)} %refs_1_.3, bf16[512,256]{1,0:T(8,128)(2,1)S(1)} %get-tuple-element.21.refs_2_, bf16[512,256]{1,0:T(8,128)(2,1)S(1)} %get-tuple-element.22.refs_3_), custom_call_target="tpu_custom_call" | custom-call | flops 536870912 | bytes 4194304 | tf_op jit(solution)/shard_map/pallas_call | solution.py:319
  15.7 0.1 collective-permute-done.2.refs_0_.payload_before
  15.8 0.0 collective-permute-done.3.refs_1_
  15.8 2.5 %shard_map.68 = (f32[2,256,256]{2,1,0:T(8,128)S(1)}, f32[256,256]{1,0:T(8,128)S(1)}) custom-call(f32[32,256]{1,0:T(8,128)S(1)} %collective-permute-done.2.refs_0_.payload_before, f32[1,1,2,256,256]{4,3,2,1,0:T(8,128)S(1)} %collective-permute-done.3.refs_1_, bf16[512,256]{1,0:T(8,128)(2,1)S(1)} %get-tuple-element.21.refs_2_, ...), custom_call_target="tpu_custom_call" | custom-call | flops 536870912 | bytes 4194304 | tf_op jit(solution)/shard_map/pallas_call | solution.py:319
  18.3 1.6 %collective-permute-start.4 = (f32[256,256]{1,0:T(8,128)S(1)}, f32[256,256]{1,0:T(8,128)S(1)}, u32[]{:S(2)}, u32[]{:S(2)}) collective-permute-start(f32[256,256]{1,0:T(8,128)S(1)} %get-tuple-element.32), channel_id=1, source_target_pairs={{0,1},{1,2},{2,3},{3,0},{4,5},{5,6},{6,7},{7,4},{8,9},{9,10},{10,1... | collective-permute-start | bytes 786440 | tf_op jit(solution)/shard_map/ppermute | solution.py:347
  19.9 2.9 %shard_map.69 = (f32[256,4096]{1,0:T(8,128)}, f32[256,256]{1,0:T(8,128)S(1)}) custom-call(f32[32,256]{1,0:T(8,128)S(1)} %concatenate.11.refs_0_.payload_in, f32[32,256]{1,0:T(8,128)S(1)} %collective-permute-done.2.refs_0_.payload_before, f32[2,256,256]{2,1,0:T(8,128)S(1)} %get-tuple-element.25.own, f32[2,256,256]{2,1,0:T(8,128)S(1)} %get-tuple-element.26.own_later, ...), custom_call_target="tpu_custom_call" | custom-call | flops 1048576 | bytes 12582912 | tf_op jit(solution)/shard_map/pallas_call | solution.py:348
  22.8 4.2 %collective-permute-done.4.across = f32[256,256]{1,0:T(8,128)S(1)} collective-permute-done((f32[256,256]{1,0:T(8,128)S(1)}, f32[256,256]{1,0:T(8,128)S(1)}, u32[]{:S(2)}, u32[]{:S(2)}) %collective-permute-start.4) | collective-permute-done | bytes 262176 | tf_op jit(solution)/shard_map/ppermute | solution.py:347
  27.0 0.7 %shard_map.70 = f32[256,4096]{1,0:T(8,128)} custom-call(f32[256,4096]{1,0:T(8,128)} %get-tuple-element.30.image_in, f32[256,256]{1,0:T(8,128)S(1)} %get-tuple-element.31.block, f32[256,256]{1,0:T(8,128)S(1)} %collective-permute-done.4.across), custom_call_target="tpu_custom_call", output_to_operand_aliasing={{}: (0, {})} | custom-call | tf_op jit(solution)/shard_map/pallas_call | solution.py:357
  (4 shorter events, 0.0 us)
Async XLA Ops:
  0.0 15.8 %collective-permute-start.3 = (f32[1,1,2,256,256]{4,3,2,1,0:T(8,128)}, f32[1,1,2,256,256]{4,3,2,1,0:T(8,128)S(1)}, u32[]{:S(2)}, u32[]{:S(2)}) collective-permute-start(f32[1,1,2,256,256]{4,3,2,1,0:T(8,128)} %refs_1_.3), channel_id=1, source_target_pairs={{0,4},{4,8},{8,12},{12,16},{16,20},{20,24},{24,28},{28,0},{1,5},{5... | collective-permute-start | bytes 1572872 | tf_op jit(solution)/shard_map/ppermute | solution.py:296
  1.3 5.3 %collective-permute-start = (f32[8,256]{1,0:T(8,128)S(1)}, f32[8,256]{1,0:T(8,128)S(1)}, u32[]{:S(2)}, u32[]{:S(2)}) collective-permute-start(f32[8,256]{1,0:T(8,128)S(1)} %pad_maximum_fusion), channel_id=1, source_target_pairs={{0,2},{1,3},{2,0},{3,1},{4,6},{5,7},{6,4},{7,5},{8,10},{9,11},{10,... | collective-permute-start | bytes 24584 | tf_op jit(solution)/shard_map/ppermute | solution.py:101
  6.6 3.7 %collective-permute-start.1 = (f32[8,256]{1,0:T(8,128)S(1)}, f32[8,256]{1,0:T(8,128)S(1)}, u32[]{:S(2)}, u32[]{:S(2)}) collective-permute-start(f32[8,256]{1,0:T(8,128)S(1)} %pad_maximum_fusion.1), channel_id=1, source_target_pairs={{0,1},{1,0},{2,3},{3,2},{4,5},{5,4},{6,7},{7,6},{8,9},{9,8},{10,11... | collective-permute-start | bytes 24584 | tf_op jit(solution)/shard_map/ppermute | solution.py:101
  8.5 0.7 %copy-start = (f32[16,256]{1,0:T(8,128)S(1)}, f32[16,256]{1,0:T(8,128)}, u32[]{:S(2)}) copy-start(f32[16,256]{1,0:T(8,128)} %shard_map.64.numbers_in) | copy-start | bytes 49156
  10.4 5.3 %collective-permute-start.2 = (f32[32,256]{1,0:T(8,128)S(1)}, f32[32,256]{1,0:T(8,128)S(1)}, u32[]{:S(2)}, u32[]{:S(2)}) collective-permute-start(f32[32,256]{1,0:T(8,128)S(1)} %concatenate.11.refs_0_.payload_in), channel_id=1, source_target_pairs={{0,4},{4,8},{8,12},{12,16},{16,20},{20,24},{24,28},{28,0},{1,5},{5... | collective-permute-start | bytes 98312 | tf_op jit(solution)/shard_map/ppermute | solution.py:342
  18.3 8.7 %collective-permute-start.4 = (f32[256,256]{1,0:T(8,128)S(1)}, f32[256,256]{1,0:T(8,128)S(1)}, u32[]{:S(2)}, u32[]{:S(2)}) collective-permute-start(f32[256,256]{1,0:T(8,128)S(1)} %get-tuple-element.32), channel_id=1, source_target_pairs={{0,1},{1,2},{2,3},{3,0},{4,5},{5,6},{6,7},{7,4},{8,9},{9,10},{10,1... | collective-permute-start | bytes 786440 | tf_op jit(solution)/shard_map/ppermute | solution.py:347

commit v5 on v4

--- a/solution.py
+++ b/solution.py
@@ -89,7 +89,7 @@
 
 
 def sender(n, me, k):
-    return me ^ (0, 2, 1, 3)[k] if n == 4 else lax.rem(me - k + n, n)
+    return me ^ k if n == 4 else lax.rem(me - k + n, n)
 
 
 def exchange(n, me, visibilities, positions, numbers):
@@ -106,10 +106,10 @@
             ring = [(i, (i + k) % n) for i in range(n)]
             pieces.append(lax.ppermute(slot(lax.rem(me + k, n)), "chan", ring))
         return pieces
-    far = swap(jnp.concatenate([slot(me ^ 2), slot(me ^ 3)], axis=0), 2)
-    far, numbers = lax.optimization_barrier((far, numbers))
-    near = swap(jnp.concatenate([slot(me ^ 1), far[4:]], axis=0), 1)
-    return [slot(me), far[:4], near]
+    near = swap(jnp.concatenate([slot(me ^ 1), slot(me ^ 3)], axis=0), 1)
+    near, numbers = lax.optimization_barrier((near, numbers))
+    far = swap(jnp.concatenate([slot(me ^ 2), near[4:]], axis=0), 2)
+    return [slot(me), near[:4], far]
 
 
 def fill_factors(n, payload, le, lo, we, wo):
@@ -282,7 +282,6 @@
     rows = visibilities.shape[-1]
     vmem = pl.BlockSpec(memory_space=pltpu.VMEM)
     anywhere = pl.BlockSpec(memory_space=pl.ANY)
-    hbm = pl.BlockSpec(memory_space=pltpu.HBM)
     facet_ring = [(i, (i + 1) % facets) for i in range(facets)]
 
     numbers = pl.pallas_call(
@@ -331,7 +330,9 @@
                 pltpu.SemaphoreType.DMA((1 + PARTS,)),
             ]
             + [pltpu.VMEM((2, SUB, SUB), jnp.float32)] * (not spilled),
-            compiler_params=pltpu.CompilerParams(vmem_limit_bytes=max(room << 20, 0 if spilled else 209 << 18)),
+            compiler_params=pltpu.CompilerParams(
+                vmem_limit_bytes=max(room << 20, 0 if spilled else 209 << 18)
+            ),
             cost_estimate=pl.CostEstimate(
                 flops=2 * depth * SUB * SUB * 4, bytes_accessed=4 << 20, transcendentals=0
             ),

time: 28 us -> 28 us (level)
  transfers between devices with their start and end apart: 5 -> 5, of which waited for: 4 -> 3; matrix products, arithmetic and copies ran while one was open for 3% -> 3% of each run, Pallas kernels for 26% -> 26%
where the time goes in v5:
time: 28 us; the launch traced here: 27.7 us
  starting transfers between devices  10.6 us (38%)
  Pallas kernels  10.5 us (38%)
  waiting for transfers between devices  5.03 us (18%)
  local copies, waits for them, and re-layouts  1.54 us (6%)
    ppermute x2, starting transfers between devices, swap(): return lax.ppermute(piece, 'chan', [(i, i ^ bit) for i in range(n)])  5.74 us
    pallas_call x3, Pallas kernels, pictures_of(): pl.pallas_call(functools.partial(picture_kernel, n, scale, turn), out_sha...  5.15 us
    ppermute x1, waiting for transfers between devices, shards(): across = lax.ppermute(across, 'chan', [(i, (i + 1) % n) for i in range(n)])  4.32 us
    pallas_call x1, Pallas kernels, shards(): pl.pallas_call(functools.partial(paste_kernel, n), out_shape=(jax.ShapeDt...  2.8 us
    ppermute x1, starting transfers between devices, shards(): payload_before = lax.ppermute(payload, 'facet', facet_ring)  2.73 us
    ppermute x1, starting transfers between devices, shards(): across = lax.ppermute(across, 'chan', [(i, (i + 1) % n) for i in range(n)])  1.63 us
    pallas_call x1, Pallas kernels, shards(): pl.pallas_call(functools.partial(numbers_kernel, n), out_shape=jax.ShapeD...  1.36 us
    squeeze x1, local copies, waits for them, and re-layouts, slot(): lax.dynamic_index_in_dim(a[0, 0], index, 0, False)  0.8 us
  transfers between devices with their start and end apart: 5, of which 3 were waited for; matrix products, arithmetic and copies ran while one was open for 3% of the time, Pallas kernels for 26%

profile of v5, /device:TPU:0, one launch (start us, length us, event | category | flops | bytes accessed | tf_op | source)
XLA Modules:
  0.0 27.7 jit_solution(13370812360990283012)
XLA Ops:
  0.0 0.5 %collective-permute-start.3 = (f32[1,1,2,256,256]{4,3,2,1,0:T(8,128)}, f32[1,1,2,256,256]{4,3,2,1,0:T(8,128)S(1)}, u32[]{:S(2)}, u32[]{:S(2)}) collective-permute-start(f32[1,1,2,256,256]{4,3,2,1,0:T(8,128)} %refs_1_.3), channel_id=1, source_target_pairs={{0,4},{4,8},{8,12},{12,16},{16,20},{20,24},{24,28},{28,0},{1,5},{5... | collective-permute-start | bytes 1572872 | tf_op jit(solution)/shard_map/ppermute | solution.py:295
  0.5 0.8 %dynamic-slice_bitcast_fusion = (f32[2,256]{1,0:T(2,128)S(1)}, f32[2,256]{1,0:T(2,128)S(1)}, f32[2,256]{1,0:T(2,128)S(1)}, f32[2,256]{1,0:T(2,128)S(1)}, f32[2,2...) fusion(f32[1,1,4,2,256]{4,3,2,1,0:T(2,128)} %param.7, s32[]{:T(128)S(6)} %select_n.20, ...), kind=kLoop, calls=%fused_computation.2 | loop fusion | bytes 32784 | tf_op jit(solution)/shard_map/jit(dynamic_index_in_dim)/squeeze | solution.py:97
  1.3 2.6 %collective-permute-start = (f32[8,256]{1,0:T(8,128)S(1)}, f32[8,256]{1,0:T(8,128)S(1)}, u32[]{:S(2)}, u32[]{:S(2)}) collective-permute-start(f32[8,256]{1,0:T(8,128)S(1)} %pad_maximum_fusion), channel_id=1, source_target_pairs={{0,1},{1,0},{2,3},{3,2},{4,5},{5,4},{6,7},{7,6},{8,9},{9,8},{10,11... | collective-permute-start | bytes 24584 | tf_op jit(solution)/shard_map/ppermute | solution.py:101
  3.9 1.4 %shard_map.64.numbers_in = f32[16,256]{1,0:T(8,128)} custom-call(s32[1,1,4,4]{3,2,1,0:T(4,128)} %tracks.1, s32[1,1,4]{2,1,0:T(1,128)} %counts.1, s32[1,1,2,2]{3,2,1,0:T(2,128)} %offsets.1), custom_call_target="tpu_custom_call" | custom-call | tf_op jit(solution)/shard_map/pallas_call | solution.py:287
  5.3 0.3 collective-permute-done
  5.6 3.1 %collective-permute-start.1 = (f32[8,256]{1,0:T(8,128)S(1)}, f32[8,256]{1,0:T(8,128)S(1)}, u32[]{:S(2)}, u32[]{:S(2)}) collective-permute-start(f32[8,256]{1,0:T(8,128)S(1)} %pad_maximum_fusion.1), channel_id=1, source_target_pairs={{0,2},{1,3},{2,0},{3,1},{4,6},{5,7},{6,4},{7,5},{8,10},{9,11},{10,... | collective-permute-start | bytes 24584 | tf_op jit(solution)/shard_map/ppermute | solution.py:101
  8.7 0.0 copy-start
  8.7 0.7 %copy-done = f32[16,256]{1,0:T(8,128)S(1)} copy-done((f32[16,256]{1,0:T(8,128)S(1)}, f32[16,256]{1,0:T(8,128)}, u32[]{:S(2)}) %copy-start) | copy-done | bytes 16408
  9.4 0.5 %shard_map.65 = (bf16[512,256]{1,0:T(8,128)(2,1)S(1)}, bf16[512,256]{1,0:T(8,128)(2,1)S(1)}, f32[16,256]{1,0:T(8,128)S(1)}) custom-call(f32[16,256]{1,0:T(8,128)S(1)} %copy-done), custom_call_target="tpu_custom_call" | custom-call | flops 4194304 | bytes 1048576 | tf_op jit(solution)/shard_map/pallas_call | solution.py:296
  9.9 0.4 %collective-permute-done.1 = f32[8,256]{1,0:T(8,128)S(1)} collective-permute-done((f32[8,256]{1,0:T(8,128)S(1)}, f32[8,256]{1,0:T(8,128)S(1)}, u32[]{:S(2)}, u32[]{:S(2)}) %collective-permute-start.1) | collective-permute-done | bytes 8224 | tf_op jit(solution)/shard_map/ppermute | solution.py:101
  10.3 0.1 shard_map.66
  10.4 2.7 %collective-permute-start.2 = (f32[32,256]{1,0:T(8,128)S(1)}, f32[32,256]{1,0:T(8,128)S(1)}, u32[]{:S(2)}, u32[]{:S(2)}) collective-permute-start(f32[32,256]{1,0:T(8,128)S(1)} %concatenate.11.refs_0_.payload_in), channel_id=1, source_target_pairs={{0,4},{4,8},{8,12},{12,16},{16,20},{20,24},{24,28},{28,0},{1,5},{5... | collective-permute-start | bytes 98312 | tf_op jit(solution)/shard_map/ppermute | solution.py:343
  13.1 2.5 %shard_map.67 = (f32[2,256,256]{2,1,0:T(8,128)S(1)}, f32[256,256]{1,0:T(8,128)S(1)}) custom-call(f32[32,256]{1,0:T(8,128)S(1)} %concatenate.11.refs_0_.payload_in, f32[1,1,2,256,256]{4,3,2,1,0:T(8,128)} %refs_1_.3, bf16[512,256]{1,0:T(8,128)(2,1)S(1)} %get-tuple-element.21.refs_2_, bf16[512,256]{1,0:T(8,128)(2,1)S(1)} %get-tuple-element.22.refs_3_), custom_call_target="tpu_custom_call" | custom-call | flops 536870912 | bytes 4194304 | tf_op jit(solution)/shard_map/pallas_call | solution.py:318
  15.7 0.0 collective-permute-done.2.refs_0_.payload_before
  15.7 0.0 collective-permute-done.3.refs_1_
  15.7 2.5 %shard_map.68 = (f32[2,256,256]{2,1,0:T(8,128)S(1)}, f32[256,256]{1,0:T(8,128)S(1)}) custom-call(f32[32,256]{1,0:T(8,128)S(1)} %collective-permute-done.2.refs_0_.payload_before, f32[1,1,2,256,256]{4,3,2,1,0:T(8,128)S(1)} %collective-permute-done.3.refs_1_, bf16[512,256]{1,0:T(8,128)(2,1)S(1)} %get-tuple-element.21.refs_2_, ...), custom_call_target="tpu_custom_call" | custom-call | flops 536870912 | bytes 4194304 | tf_op jit(solution)/shard_map/pallas_call | solution.py:318
  18.2 1.6 %collective-permute-start.4 = (f32[256,256]{1,0:T(8,128)S(1)}, f32[256,256]{1,0:T(8,128)S(1)}, u32[]{:S(2)}, u32[]{:S(2)}) collective-permute-start(f32[256,256]{1,0:T(8,128)S(1)} %get-tuple-element.32), channel_id=1, source_target_pairs={{0,1},{1,2},{2,3},{3,0},{4,5},{5,6},{6,7},{7,4},{8,9},{9,10},{10,1... | collective-permute-start | bytes 786440 | tf_op jit(solution)/shard_map/ppermute | solution.py:348
  19.9 2.8 %shard_map.69 = (f32[256,4096]{1,0:T(8,128)}, f32[256,256]{1,0:T(8,128)S(1)}) custom-call(f32[32,256]{1,0:T(8,128)S(1)} %concatenate.11.refs_0_.payload_in, f32[32,256]{1,0:T(8,128)S(1)} %collective-permute-done.2.refs_0_.payload_before, f32[2,256,256]{2,1,0:T(8,128)S(1)} %get-tuple-element.25.own, f32[2,256,256]{2,1,0:T(8,128)S(1)} %get-tuple-element.26.own_later, ...), custom_call_target="tpu_custom_call" | custom-call | flops 1048576 | bytes 12582912 | tf_op jit(solution)/shard_map/pallas_call | solution.py:349
  22.7 4.3 %collective-permute-done.4.across = f32[256,256]{1,0:T(8,128)S(1)} collective-permute-done((f32[256,256]{1,0:T(8,128)S(1)}, f32[256,256]{1,0:T(8,128)S(1)}, u32[]{:S(2)}, u32[]{:S(2)}) %collective-permute-start.4) | collective-permute-done | bytes 262176 | tf_op jit(solution)/shard_map/ppermute | solution.py:348
  27.0 0.7 %shard_map.70 = f32[256,4096]{1,0:T(8,128)} custom-call(f32[256,4096]{1,0:T(8,128)} %get-tuple-element.30.image_in, f32[256,256]{1,0:T(8,128)S(1)} %get-tuple-element.31.block, f32[256,256]{1,0:T(8,128)S(1)} %collective-permute-done.4.across), custom_call_target="tpu_custom_call", output_to_operand_aliasing={{}: (0, {})} | custom-call | tf_op jit(solution)/shard_map/pallas_call | solution.py:358
  (4 shorter events, 0.0 us)
Async XLA Ops:
  0.0 15.7 %collective-permute-start.3 = (f32[1,1,2,256,256]{4,3,2,1,0:T(8,128)}, f32[1,1,2,256,256]{4,3,2,1,0:T(8,128)S(1)}, u32[]{:S(2)}, u32[]{:S(2)}) collective-permute-start(f32[1,1,2,256,256]{4,3,2,1,0:T(8,128)} %refs_1_.3), channel_id=1, source_target_pairs={{0,4},{4,8},{8,12},{12,16},{16,20},{20,24},{24,28},{28,0},{1,5},{5... | collective-permute-start | bytes 1572872 | tf_op jit(solution)/shard_map/ppermute | solution.py:295
  1.3 4.3 %collective-permute-start = (f32[8,256]{1,0:T(8,128)S(1)}, f32[8,256]{1,0:T(8,128)S(1)}, u32[]{:S(2)}, u32[]{:S(2)}) collective-permute-start(f32[8,256]{1,0:T(8,128)S(1)} %pad_maximum_fusion), channel_id=1, source_target_pairs={{0,1},{1,0},{2,3},{3,2},{4,5},{5,4},{6,7},{7,6},{8,9},{9,8},{10,11... | collective-permute-start | bytes 24584 | tf_op jit(solution)/shard_map/ppermute | solution.py:101
  5.6 4.7 %collective-permute-start.1 = (f32[8,256]{1,0:T(8,128)S(1)}, f32[8,256]{1,0:T(8,128)S(1)}, u32[]{:S(2)}, u32[]{:S(2)}) collective-permute-start(f32[8,256]{1,0:T(8,128)S(1)} %pad_maximum_fusion.1), channel_id=1, source_target_pairs={{0,2},{1,3},{2,0},{3,1},{4,6},{5,7},{6,4},{7,5},{8,10},{9,11},{10,... | collective-permute-start | bytes 24584 | tf_op jit(solution)/shard_map/ppermute | solution.py:101
  8.7 0.7 %copy-start = (f32[16,256]{1,0:T(8,128)S(1)}, f32[16,256]{1,0:T(8,128)}, u32[]{:S(2)}) copy-start(f32[16,256]{1,0:T(8,128)} %shard_map.64.numbers_in) | copy-start | bytes 49156
  10.4 5.3 %collective-permute-start.2 = (f32[32,256]{1,0:T(8,128)S(1)}, f32[32,256]{1,0:T(8,128)S(1)}, u32[]{:S(2)}, u32[]{:S(2)}) collective-permute-start(f32[32,256]{1,0:T(8,128)S(1)} %concatenate.11.refs_0_.payload_in), channel_id=1, source_target_pairs={{0,4},{4,8},{8,12},{12,16},{16,20},{20,24},{24,28},{28,0},{1,5},{5... | collective-permute-start | bytes 98312 | tf_op jit(solution)/shard_map/ppermute | solution.py:343
  18.2 8.8 %collective-permute-start.4 = (f32[256,256]{1,0:T(8,128)S(1)}, f32[256,256]{1,0:T(8,128)S(1)}, u32[]{:S(2)}, u32[]{:S(2)}) collective-permute-start(f32[256,256]{1,0:T(8,128)S(1)} %get-tuple-element.32), channel_id=1, source_target_pairs={{0,1},{1,2},{2,3},{3,0},{4,5},{5,6},{6,7},{7,4},{8,9},{9,10},{10,1... | collective-permute-start | bytes 786440 | tf_op jit(solution)/shard_map/ppermute | solution.py:348

commit v6 on v5

--- a/solution.py
+++ b/solution.py
@@ -29,11 +29,11 @@
         target = jnp.zeros_like(lane)
         for b in range(tracks.shape[-1]):
             target = jnp.where(block == b, tracks[0, 0, source, b], target)
-        lines += [target, jnp.where(block < counts[0, 0, source], 1, 0)]
+        lines.append(jnp.where(block < counts[0, 0, source], target + 1, 0))
     corners = jnp.zeros_like(lane)
     for place in range(4):
         corners = jnp.where(lane == place, offsets[0, 0, place // 2, place % 2], corners)
-    lines += [corners] * (out.shape[0] - 2 * n)
+    lines = [corners] + lines + [corners] * (out.shape[0] - n - 1)
     out[...] = jnp.concatenate(lines, axis=0).astype(jnp.float32)
 
 
@@ -118,10 +118,9 @@
     zero = jnp.zeros((TILE, rows), jnp.bfloat16)
     for k in range(n):
         piece = payload[4 * k : 4 * k + 4]
-        target = payload[4 * n + 2 * k : 4 * n + 2 * k + 1]
-        live = payload[4 * n + 2 * k + 1 : 4 * n + 2 * k + 2]
-        real = piece[0:1] * live
-        imag = piece[1:2] * live
+        target = payload[4 * n + 1 + k : 4 * n + 2 + k]
+        real = jnp.where(target > 0.0, piece[0:1], 0.0)
+        imag = jnp.where(target > 0.0, piece[1:2], 0.0)
         u_position = piece[2:3]
         u_even, u_odd, u_turn = folded(u_position, rho)
         v_even, v_odd, v_turn = folded(piece[3:4], rho)
@@ -133,7 +132,7 @@
                 start = part * (ref.shape[0] // 2) + row
                 ref[start : start + TILE, place] = value
 
-        first = target == 0.0
+        first = target < 2.0
         evens = [halves(jnp.where(first, u_even, 0.0)), halves(jnp.where(first, 0.0, u_even))]
         odds = [halves(jnp.where(first, u_odd, 0.0)), halves(jnp.where(first, 0.0, u_odd))]
         for turn in range(HALF // TILE):
@@ -192,7 +191,7 @@
     payload, screens_in, ahead, behind = refs[:4]
     pictures, across = refs[count : count + 2]
     corners, le, lo, we, wo, sems = refs[count + 2 : count + 8]
-    copies = [pltpu.make_async_copy(payload.at[pl.ds(6 * n, 1)], corners, sems.at[0])]
+    copies = [pltpu.make_async_copy(payload.at[pl.ds(4 * n, 1)], corners, sems.at[0])]
     if spilled:
         screens = screens_in.at[0, 0]
     else:
@@ -243,7 +242,7 @@
 
 def paste_kernel(n, payload_in, payload_before, own, own_later, before, out, block_out, corners, sems):
     copies = [
-        pltpu.make_async_copy(source.at[pl.ds(6 * n, 1)], corners.at[pl.ds(i, 1)], sems.at[i])
+        pltpu.make_async_copy(source.at[pl.ds(4 * n, 1)], corners.at[pl.ds(i, 1)], sems.at[i])
         for i, source in enumerate((payload_in, payload_before))
     ]
     for copy in copies:
@@ -282,11 +281,12 @@
     rows = visibilities.shape[-1]
     vmem = pl.BlockSpec(memory_space=pltpu.VMEM)
     anywhere = pl.BlockSpec(memory_space=pl.ANY)
+    lines = n // 8 * 8 + 8
     facet_ring = [(i, (i + 1) % facets) for i in range(facets)]
 
     numbers = pl.pallas_call(
         functools.partial(numbers_kernel, n),
-        out_shape=jax.ShapeDtypeStruct((2 * n + 8, rows), jnp.float32),
+        out_shape=jax.ShapeDtypeStruct((lines, rows), jnp.float32),
         in_specs=[pl.BlockSpec(memory_space=pltpu.SMEM)] * 3,
         out_specs=vmem,
         compiler_params=pltpu.CompilerParams(vmem_limit_bytes=56 << 20),
@@ -298,7 +298,7 @@
         out_shape=(
             jax.ShapeDtypeStruct((2 * SUB, SUB), jnp.bfloat16),
             jax.ShapeDtypeStruct((2 * SUB, SUB), jnp.bfloat16),
-            jax.ShapeDtypeStruct((2 * n + 8, rows), jnp.float32),
+            jax.ShapeDtypeStruct((lines, rows), jnp.float32),
         ),
         in_specs=[vmem],
         out_specs=(vmem, vmem, vmem),

time: 28 us -> 28 us (level)
  no operation moved by 1% of the time
where the time goes in v6:
time: 28 us; the launch traced here: 27.7 us
  Pallas kernels  10.6 us (38%)
  starting transfers between devices  10.5 us (38%)
  waiting for transfers between devices  5 us (18%)
  local copies, waits for them, and re-layouts  1.52 us (5%)
    ppermute x2, starting transfers between devices, swap(): return lax.ppermute(piece, 'chan', [(i, i ^ bit) for i in range(n)])  5.74 us
    pallas_call x3, Pallas kernels, pictures_of(): pl.pallas_call(functools.partial(picture_kernel, n, scale, turn), out_sha...  5.15 us
    ppermute x1, waiting for transfers between devices, shards(): across = lax.ppermute(across, 'chan', [(i, (i + 1) % n) for i in range(n)])  4.27 us
    pallas_call x1, Pallas kernels, shards(): pl.pallas_call(functools.partial(paste_kernel, n), out_shape=(jax.ShapeDt...  2.85 us
    ppermute x1, starting transfers between devices, shards(): payload_before = lax.ppermute(payload, 'facet', facet_ring)  2.73 us
    ppermute x1, starting transfers between devices, shards(): across = lax.ppermute(across, 'chan', [(i, (i + 1) % n) for i in range(n)])  1.63 us
    pallas_call x1, Pallas kernels, shards(): pl.pallas_call(functools.partial(numbers_kernel, n), out_shape=jax.ShapeD...  1.35 us
    squeeze x1, local copies, waits for them, and re-layouts, slot(): lax.dynamic_index_in_dim(a[0, 0], index, 0, False)  0.8 us
  transfers between devices with their start and end apart: 5, of which 3 were waited for; matrix products, arithmetic and copies ran while one was open for 3% of the time, Pallas kernels for 26%

profile of v6, /device:TPU:0, one launch (start us, length us, event | category | flops | bytes accessed | tf_op | source)
XLA Modules:
  0.0 27.7 jit_solution(3954981639687999171)
XLA Ops:
  0.0 0.5 %collective-permute-start.3 = (f32[1,1,2,256,256]{4,3,2,1,0:T(8,128)}, f32[1,1,2,256,256]{4,3,2,1,0:T(8,128)S(1)}, u32[]{:S(2)}, u32[]{:S(2)}) collective-permute-start(f32[1,1,2,256,256]{4,3,2,1,0:T(8,128)} %refs_1_.3), channel_id=1, source_target_pairs={{0,4},{4,8},{8,12},{12,16},{16,20},{20,24},{24,28},{28,0},{1,5},{5... | collective-permute-start | bytes 1572872 | tf_op jit(solution)/shard_map/ppermute | solution.py:295
  0.5 0.8 %dynamic-slice_bitcast_fusion = (f32[2,256]{1,0:T(2,128)S(1)}, f32[2,256]{1,0:T(2,128)S(1)}, f32[2,256]{1,0:T(2,128)S(1)}, f32[2,256]{1,0:T(2,128)S(1)}, f32[2,2...) fusion(f32[1,1,4,2,256]{4,3,2,1,0:T(2,128)} %param.7, s32[]{:T(128)S(6)} %select_n.20, ...), kind=kLoop, calls=%fused_computation.2 | loop fusion | bytes 32784 | tf_op jit(solution)/shard_map/jit(dynamic_index_in_dim)/squeeze | solution.py:97
  1.3 2.6 %collective-permute-start = (f32[8,256]{1,0:T(8,128)S(1)}, f32[8,256]{1,0:T(8,128)S(1)}, u32[]{:S(2)}, u32[]{:S(2)}) collective-permute-start(f32[8,256]{1,0:T(8,128)S(1)} %pad_maximum_fusion), channel_id=1, source_target_pairs={{0,1},{1,0},{2,3},{3,2},{4,5},{5,4},{6,7},{7,6},{8,9},{9,8},{10,11... | collective-permute-start | bytes 24584 | tf_op jit(solution)/shard_map/ppermute | solution.py:101
  3.9 1.4 %shard_map.64.numbers_in = f32[8,256]{1,0:T(8,128)} custom-call(s32[1,1,4,4]{3,2,1,0:T(4,128)} %tracks.1, s32[1,1,4]{2,1,0:T(1,128)} %counts.1, s32[1,1,2,2]{3,2,1,0:T(2,128)} %offsets.1), custom_call_target="tpu_custom_call" | custom-call | tf_op jit(solution)/shard_map/pallas_call | solution.py:287
  5.3 0.3 %collective-permute-done = f32[8,256]{1,0:T(8,128)S(1)} collective-permute-done((f32[8,256]{1,0:T(8,128)S(1)}, f32[8,256]{1,0:T(8,128)S(1)}, u32[]{:S(2)}, u32[]{:S(2)}) %collective-permute-start) | collective-permute-done | bytes 8224 | tf_op jit(solution)/shard_map/ppermute | solution.py:101
  5.6 3.1 %collective-permute-start.1 = (f32[8,256]{1,0:T(8,128)S(1)}, f32[8,256]{1,0:T(8,128)S(1)}, u32[]{:S(2)}, u32[]{:S(2)}) collective-permute-start(f32[8,256]{1,0:T(8,128)S(1)} %pad_maximum_fusion.1), channel_id=1, source_target_pairs={{0,2},{1,3},{2,0},{3,1},{4,6},{5,7},{6,4},{7,5},{8,10},{9,11},{10,... | collective-permute-start | bytes 24584 | tf_op jit(solution)/shard_map/ppermute | solution.py:101
  8.7 0.0 copy-start
  8.7 0.7 %copy-done = f32[8,256]{1,0:T(8,128)S(1)} copy-done((f32[8,256]{1,0:T(8,128)S(1)}, f32[8,256]{1,0:T(8,128)}, u32[]{:S(2)}) %copy-start) | copy-done | bytes 8216
  9.3 0.5 %shard_map.65 = (bf16[512,256]{1,0:T(8,128)(2,1)S(1)}, bf16[512,256]{1,0:T(8,128)(2,1)S(1)}, f32[8,256]{1,0:T(8,128)S(1)}) custom-call(f32[8,256]{1,0:T(8,128)S(1)} %copy-done), custom_call_target="tpu_custom_call" | custom-call | flops 4194304 | bytes 1048576 | tf_op jit(solution)/shard_map/pallas_call | solution.py:296
  9.8 0.4 %collective-permute-done.1 = f32[8,256]{1,0:T(8,128)S(1)} collective-permute-done((f32[8,256]{1,0:T(8,128)S(1)}, f32[8,256]{1,0:T(8,128)S(1)}, u32[]{:S(2)}, u32[]{:S(2)}) %collective-permute-start.1) | collective-permute-done | bytes 8224 | tf_op jit(solution)/shard_map/ppermute | solution.py:101
  10.3 0.1 shard_map.66
  10.4 2.7 %collective-permute-start.2 = (f32[24,256]{1,0:T(8,128)S(1)}, f32[24,256]{1,0:T(8,128)S(1)}, u32[]{:S(2)}, u32[]{:S(2)}) collective-permute-start(f32[24,256]{1,0:T(8,128)S(1)} %concatenate.11.refs_0_.payload_in), channel_id=1, source_target_pairs={{0,4},{4,8},{8,12},{12,16},{16,20},{20,24},{24,28},{28,0},{1,5},{5... | collective-permute-start | bytes 73736 | tf_op jit(solution)/shard_map/ppermute | solution.py:343
  13.1 2.5 %shard_map.67 = (f32[2,256,256]{2,1,0:T(8,128)S(1)}, f32[256,256]{1,0:T(8,128)S(1)}) custom-call(f32[24,256]{1,0:T(8,128)S(1)} %concatenate.11.refs_0_.payload_in, f32[1,1,2,256,256]{4,3,2,1,0:T(8,128)} %refs_1_.3, bf16[512,256]{1,0:T(8,128)(2,1)S(1)} %get-tuple-element.21.refs_2_, bf16[512,256]{1,0:T(8,128)(2,1)S(1)} %get-tuple-element.22.refs_3_), custom_call_target="tpu_custom_call" | custom-call | flops 536870912 | bytes 4194304 | tf_op jit(solution)/shard_map/pallas_call | solution.py:318
  15.7 0.0 collective-permute-done.2.refs_0_.payload_before
  15.7 0.0 collective-permute-done.3.refs_1_
  15.7 2.5 %shard_map.68 = (f32[2,256,256]{2,1,0:T(8,128)S(1)}, f32[256,256]{1,0:T(8,128)S(1)}) custom-call(f32[24,256]{1,0:T(8,128)S(1)} %collective-permute-done.2.refs_0_.payload_before, f32[1,1,2,256,256]{4,3,2,1,0:T(8,128)S(1)} %collective-permute-done.3.refs_1_, bf16[512,256]{1,0:T(8,128)(2,1)S(1)} %get-tuple-element.21.refs_2_, ...), custom_call_target="tpu_custom_call" | custom-call | flops 536870912 | bytes 4194304 | tf_op jit(solution)/shard_map/pallas_call | solution.py:318
  18.2 1.6 %collective-permute-start.4 = (f32[256,256]{1,0:T(8,128)S(1)}, f32[256,256]{1,0:T(8,128)S(1)}, u32[]{:S(2)}, u32[]{:S(2)}) collective-permute-start(f32[256,256]{1,0:T(8,128)S(1)} %get-tuple-element.32), channel_id=1, source_target_pairs={{0,1},{1,2},{2,3},{3,0},{4,5},{5,6},{6,7},{7,4},{8,9},{9,10},{10,1... | collective-permute-start | bytes 786440 | tf_op jit(solution)/shard_map/ppermute | solution.py:348
  19.9 2.8 %shard_map.69 = (f32[256,4096]{1,0:T(8,128)}, f32[256,256]{1,0:T(8,128)S(1)}) custom-call(f32[24,256]{1,0:T(8,128)S(1)} %concatenate.11.refs_0_.payload_in, f32[24,256]{1,0:T(8,128)S(1)} %collective-permute-done.2.refs_0_.payload_before, f32[2,256,256]{2,1,0:T(8,128)S(1)} %get-tuple-element.25.own, f32[2,256,256]{2,1,0:T(8,128)S(1)} %get-tuple-element.26.own_later, ...), custom_call_target="tpu_custom_call" | custom-call | flops 1048576 | bytes 12582912 | tf_op jit(solution)/shard_map/pallas_call | solution.py:349
  22.7 4.3 %collective-permute-done.4.across = f32[256,256]{1,0:T(8,128)S(1)} collective-permute-done((f32[256,256]{1,0:T(8,128)S(1)}, f32[256,256]{1,0:T(8,128)S(1)}, u32[]{:S(2)}, u32[]{:S(2)}) %collective-permute-start.4) | collective-permute-done | bytes 262176 | tf_op jit(solution)/shard_map/ppermute | solution.py:348
  27.0 0.7 %shard_map.70 = f32[256,4096]{1,0:T(8,128)} custom-call(f32[256,4096]{1,0:T(8,128)} %get-tuple-element.30.image_in, f32[256,256]{1,0:T(8,128)S(1)} %get-tuple-element.31.block, f32[256,256]{1,0:T(8,128)S(1)} %collective-permute-done.4.across), custom_call_target="tpu_custom_call", output_to_operand_aliasing={{}: (0, {})} | custom-call | tf_op jit(solution)/shard_map/pallas_call | solution.py:358
  (4 shorter events, 0.0 us)
Async XLA Ops:
  0.0 15.7 %collective-permute-start.3 = (f32[1,1,2,256,256]{4,3,2,1,0:T(8,128)}, f32[1,1,2,256,256]{4,3,2,1,0:T(8,128)S(1)}, u32[]{:S(2)}, u32[]{:S(2)}) collective-permute-start(f32[1,1,2,256,256]{4,3,2,1,0:T(8,128)} %refs_1_.3), channel_id=1, source_target_pairs={{0,4},{4,8},{8,12},{12,16},{16,20},{20,24},{24,28},{28,0},{1,5},{5... | collective-permute-start | bytes 1572872 | tf_op jit(solution)/shard_map/ppermute | solution.py:295
  1.3 4.3 %collective-permute-start = (f32[8,256]{1,0:T(8,128)S(1)}, f32[8,256]{1,0:T(8,128)S(1)}, u32[]{:S(2)}, u32[]{:S(2)}) collective-permute-start(f32[8,256]{1,0:T(8,128)S(1)} %pad_maximum_fusion), channel_id=1, source_target_pairs={{0,1},{1,0},{2,3},{3,2},{4,5},{5,4},{6,7},{7,6},{8,9},{9,8},{10,11... | collective-permute-start | bytes 24584 | tf_op jit(solution)/shard_map/ppermute | solution.py:101
  5.6 4.7 %collective-permute-start.1 = (f32[8,256]{1,0:T(8,128)S(1)}, f32[8,256]{1,0:T(8,128)S(1)}, u32[]{:S(2)}, u32[]{:S(2)}) collective-permute-start(f32[8,256]{1,0:T(8,128)S(1)} %pad_maximum_fusion.1), channel_id=1, source_target_pairs={{0,2},{1,3},{2,0},{3,1},{4,6},{5,7},{6,4},{7,5},{8,10},{9,11},{10,... | collective-permute-start | bytes 24584 | tf_op jit(solution)/shard_map/ppermute | solution.py:101
  8.7 0.7 %copy-start = (f32[8,256]{1,0:T(8,128)S(1)}, f32[8,256]{1,0:T(8,128)}, u32[]{:S(2)}) copy-start(f32[8,256]{1,0:T(8,128)} %shard_map.64.numbers_in) | copy-start | bytes 24580
  10.4 5.3 %collective-permute-start.2 = (f32[24,256]{1,0:T(8,128)S(1)}, f32[24,256]{1,0:T(8,128)S(1)}, u32[]{:S(2)}, u32[]{:S(2)}) collective-permute-start(f32[24,256]{1,0:T(8,128)S(1)} %concatenate.11.refs_0_.payload_in), channel_id=1, source_target_pairs={{0,4},{4,8},{8,12},{12,16},{16,20},{20,24},{24,28},{28,0},{1,5},{5... | collective-permute-start | bytes 73736 | tf_op jit(solution)/shard_map/ppermute | solution.py:343
  18.2 8.8 %collective-permute-start.4 = (f32[256,256]{1,0:T(8,128)S(1)}, f32[256,256]{1,0:T(8,128)S(1)}, u32[]{:S(2)}, u32[]{:S(2)}) collective-permute-start(f32[256,256]{1,0:T(8,128)S(1)} %get-tuple-element.32), channel_id=1, source_target_pairs={{0,1},{1,2},{2,3},{3,0},{4,5},{5,6},{6,7},{7,4},{8,9},{9,10},{10,1... | collective-permute-start | bytes 786440 | tf_op jit(solution)/shard_map/ppermute | solution.py:348

commit v7 on v6

--- a/solution.py
+++ b/solution.py
@@ -16,7 +16,7 @@
 BLOCK = 64
 TILE = 16
 LAST = BAND // SUB - 1
-PARTS = 8
+PARTS = 2
 
 
 def numbers_kernel(n, tracks, counts, offsets, out):

time: 28 us -> 27.9 us (level)
  no operation moved by 1% of the time
where the time goes in v7:
time: 27.9 us; the launch traced here: 27.6 us
  starting transfers between devices  10.5 us (38%)
  Pallas kernels  10.4 us (37%)
  waiting for transfers between devices  5.06 us (18%)
  local copies, waits for them, and re-layouts  1.52 us (5%)
    ppermute x2, starting transfers between devices, swap(): return lax.ppermute(piece, 'chan', [(i, i ^ bit) for i in range(n)])  5.74 us
    pallas_call x3, Pallas kernels, pictures_of(): pl.pallas_call(functools.partial(picture_kernel, n, scale, turn), out_sha...  4.98 us
    ppermute x1, waiting for transfers between devices, shards(): across = lax.ppermute(across, 'chan', [(i, (i + 1) % n) for i in range(n)])  4.33 us
    pallas_call x1, Pallas kernels, shards(): pl.pallas_call(functools.partial(paste_kernel, n), out_shape=(jax.ShapeDt...  2.85 us
    ppermute x1, starting transfers between devices, shards(): payload_before = lax.ppermute(payload, 'facet', facet_ring)  2.72 us
    ppermute x1, starting transfers between devices, shards(): across = lax.ppermute(across, 'chan', [(i, (i + 1) % n) for i in range(n)])  1.63 us
    pallas_call x1, Pallas kernels, shards(): pl.pallas_call(functools.partial(numbers_kernel, n), out_shape=jax.ShapeD...  1.35 us
    squeeze x1, local copies, waits for them, and re-layouts, slot(): lax.dynamic_index_in_dim(a[0, 0], index, 0, False)  0.8 us
  transfers between devices with their start and end apart: 5, of which 3 were waited for; matrix products, arithmetic and copies ran while one was open for 3% of the time, Pallas kernels for 26%

profile of v7, /device:TPU:0, one launch (start us, length us, event | category | flops | bytes accessed | tf_op | source)
XLA Modules:
  0.0 27.6 jit_solution(4391181323180360761)
XLA Ops:
  0.0 0.5 %collective-permute-start.3 = (f32[1,1,2,256,256]{4,3,2,1,0:T(8,128)}, f32[1,1,2,256,256]{4,3,2,1,0:T(8,128)S(1)}, u32[]{:S(2)}, u32[]{:S(2)}) collective-permute-start(f32[1,1,2,256,256]{4,3,2,1,0:T(8,128)} %refs_1_.3), channel_id=1, source_target_pairs={{0,4},{4,8},{8,12},{12,16},{16,20},{20,24},{24,28},{28,0},{1,5},{5... | collective-permute-start | bytes 1572872 | tf_op jit(solution)/shard_map/ppermute | solution.py:295
  0.5 0.8 %dynamic-slice_bitcast_fusion = (f32[2,256]{1,0:T(2,128)S(1)}, f32[2,256]{1,0:T(2,128)S(1)}, f32[2,256]{1,0:T(2,128)S(1)}, f32[2,256]{1,0:T(2,128)S(1)}, f32[2,2...) fusion(f32[1,1,4,2,256]{4,3,2,1,0:T(2,128)} %param.7, s32[]{:T(128)S(6)} %select_n.20, ...), kind=kLoop, calls=%fused_computation.2 | loop fusion | bytes 32784 | tf_op jit(solution)/shard_map/jit(dynamic_index_in_dim)/squeeze | solution.py:97
  1.3 2.6 %collective-permute-start = (f32[8,256]{1,0:T(8,128)S(1)}, f32[8,256]{1,0:T(8,128)S(1)}, u32[]{:S(2)}, u32[]{:S(2)}) collective-permute-start(f32[8,256]{1,0:T(8,128)S(1)} %pad_maximum_fusion), channel_id=1, source_target_pairs={{0,1},{1,0},{2,3},{3,2},{4,5},{5,4},{6,7},{7,6},{8,9},{9,8},{10,11... | collective-permute-start | bytes 24584 | tf_op jit(solution)/shard_map/ppermute | solution.py:101
  3.9 1.4 %shard_map.64.numbers_in = f32[8,256]{1,0:T(8,128)} custom-call(s32[1,1,4,4]{3,2,1,0:T(4,128)} %tracks.1, s32[1,1,4]{2,1,0:T(1,128)} %counts.1, s32[1,1,2,2]{3,2,1,0:T(2,128)} %offsets.1), custom_call_target="tpu_custom_call" | custom-call | tf_op jit(solution)/shard_map/pallas_call | solution.py:287
  5.3 0.3 %collective-permute-done = f32[8,256]{1,0:T(8,128)S(1)} collective-permute-done((f32[8,256]{1,0:T(8,128)S(1)}, f32[8,256]{1,0:T(8,128)S(1)}, u32[]{:S(2)}, u32[]{:S(2)}) %collective-permute-start) | collective-permute-done | bytes 8224 | tf_op jit(solution)/shard_map/ppermute | solution.py:101
  5.6 3.1 %collective-permute-start.1 = (f32[8,256]{1,0:T(8,128)S(1)}, f32[8,256]{1,0:T(8,128)S(1)}, u32[]{:S(2)}, u32[]{:S(2)}) collective-permute-start(f32[8,256]{1,0:T(8,128)S(1)} %pad_maximum_fusion.1), channel_id=1, source_target_pairs={{0,2},{1,3},{2,0},{3,1},{4,6},{5,7},{6,4},{7,5},{8,10},{9,11},{10,... | collective-permute-start | bytes 24584 | tf_op jit(solution)/shard_map/ppermute | solution.py:101
  8.7 0.0 copy-start
  8.7 0.7 %copy-done = f32[8,256]{1,0:T(8,128)S(1)} copy-done((f32[8,256]{1,0:T(8,128)S(1)}, f32[8,256]{1,0:T(8,128)}, u32[]{:S(2)}) %copy-start) | copy-done | bytes 8216
  9.3 0.5 %shard_map.65 = (bf16[512,256]{1,0:T(8,128)(2,1)S(1)}, bf16[512,256]{1,0:T(8,128)(2,1)S(1)}, f32[8,256]{1,0:T(8,128)S(1)}) custom-call(f32[8,256]{1,0:T(8,128)S(1)} %copy-done), custom_call_target="tpu_custom_call" | custom-call | flops 4194304 | bytes 1048576 | tf_op jit(solution)/shard_map/pallas_call | solution.py:296
  9.8 0.4 %collective-permute-done.1 = f32[8,256]{1,0:T(8,128)S(1)} collective-permute-done((f32[8,256]{1,0:T(8,128)S(1)}, f32[8,256]{1,0:T(8,128)S(1)}, u32[]{:S(2)}, u32[]{:S(2)}) %collective-permute-start.1) | collective-permute-done | bytes 8224 | tf_op jit(solution)/shard_map/ppermute | solution.py:101
  10.4 2.7 %collective-permute-start.2 = (f32[24,256]{1,0:T(8,128)S(1)}, f32[24,256]{1,0:T(8,128)S(1)}, u32[]{:S(2)}, u32[]{:S(2)}) collective-permute-start(f32[24,256]{1,0:T(8,128)S(1)} %concatenate.11.refs_0_.payload_in), channel_id=1, source_target_pairs={{0,4},{4,8},{8,12},{12,16},{16,20},{20,24},{24,28},{28,0},{1,5},{5... | collective-permute-start | bytes 73736 | tf_op jit(solution)/shard_map/ppermute | solution.py:343
  13.1 2.5 %shard_map.67 = (f32[2,256,256]{2,1,0:T(8,128)S(1)}, f32[256,256]{1,0:T(8,128)S(1)}) custom-call(f32[24,256]{1,0:T(8,128)S(1)} %concatenate.11.refs_0_.payload_in, f32[1,1,2,256,256]{4,3,2,1,0:T(8,128)} %refs_1_.3, bf16[512,256]{1,0:T(8,128)(2,1)S(1)} %get-tuple-element.21.refs_2_, bf16[512,256]{1,0:T(8,128)(2,1)S(1)} %get-tuple-element.22.refs_3_), custom_call_target="tpu_custom_call" | custom-call | flops 536870912 | bytes 4194304 | tf_op jit(solution)/shard_map/pallas_call | solution.py:318
  15.6 0.0 collective-permute-done.2.refs_0_.payload_before
  15.6 0.0 collective-permute-done.3.refs_1_
  15.6 2.5 %shard_map.68 = (f32[2,256,256]{2,1,0:T(8,128)S(1)}, f32[256,256]{1,0:T(8,128)S(1)}) custom-call(f32[24,256]{1,0:T(8,128)S(1)} %collective-permute-done.2.refs_0_.payload_before, f32[1,1,2,256,256]{4,3,2,1,0:T(8,128)S(1)} %collective-permute-done.3.refs_1_, bf16[512,256]{1,0:T(8,128)(2,1)S(1)} %get-tuple-element.21.refs_2_, ...), custom_call_target="tpu_custom_call" | custom-call | flops 536870912 | bytes 4194304 | tf_op jit(solution)/shard_map/pallas_call | solution.py:318
  18.1 1.6 %collective-permute-start.4 = (f32[256,256]{1,0:T(8,128)S(1)}, f32[256,256]{1,0:T(8,128)S(1)}, u32[]{:S(2)}, u32[]{:S(2)}) collective-permute-start(f32[256,256]{1,0:T(8,128)S(1)} %get-tuple-element.32), channel_id=1, source_target_pairs={{0,1},{1,2},{2,3},{3,0},{4,5},{5,6},{6,7},{7,4},{8,9},{9,10},{10,1... | collective-permute-start | bytes 786440 | tf_op jit(solution)/shard_map/ppermute | solution.py:348
  19.7 2.9 %shard_map.69 = (f32[256,4096]{1,0:T(8,128)}, f32[256,256]{1,0:T(8,128)S(1)}) custom-call(f32[24,256]{1,0:T(8,128)S(1)} %concatenate.11.refs_0_.payload_in, f32[24,256]{1,0:T(8,128)S(1)} %collective-permute-done.2.refs_0_.payload_before, f32[2,256,256]{2,1,0:T(8,128)S(1)} %get-tuple-element.25.own, f32[2,256,256]{2,1,0:T(8,128)S(1)} %get-tuple-element.26.own_later, ...), custom_call_target="tpu_custom_call" | custom-call | flops 1048576 | bytes 12582912 | tf_op jit(solution)/shard_map/pallas_call | solution.py:349
  22.5 4.3 %collective-permute-done.4.across = f32[256,256]{1,0:T(8,128)S(1)} collective-permute-done((f32[256,256]{1,0:T(8,128)S(1)}, f32[256,256]{1,0:T(8,128)S(1)}, u32[]{:S(2)}, u32[]{:S(2)}) %collective-permute-start.4) | collective-permute-done | bytes 262176 | tf_op jit(solution)/shard_map/ppermute | solution.py:348
  26.9 0.7 %shard_map.70 = f32[256,4096]{1,0:T(8,128)} custom-call(f32[256,4096]{1,0:T(8,128)} %get-tuple-element.30.image_in, f32[256,256]{1,0:T(8,128)S(1)} %get-tuple-element.31.block, f32[256,256]{1,0:T(8,128)S(1)} %collective-permute-done.4.across), custom_call_target="tpu_custom_call", output_to_operand_aliasing={{}: (0, {})} | custom-call | tf_op jit(solution)/shard_map/pallas_call | solution.py:358
  (5 shorter events, 0.1 us)
Async XLA Ops:
  0.0 15.6 %collective-permute-start.3 = (f32[1,1,2,256,256]{4,3,2,1,0:T(8,128)}, f32[1,1,2,256,256]{4,3,2,1,0:T(8,128)S(1)}, u32[]{:S(2)}, u32[]{:S(2)}) collective-permute-start(f32[1,1,2,256,256]{4,3,2,1,0:T(8,128)} %refs_1_.3), channel_id=1, source_target_pairs={{0,4},{4,8},{8,12},{12,16},{16,20},{20,24},{24,28},{28,0},{1,5},{5... | collective-permute-start | bytes 1572872 | tf_op jit(solution)/shard_map/ppermute | solution.py:295
  1.3 4.3 %collective-permute-start = (f32[8,256]{1,0:T(8,128)S(1)}, f32[8,256]{1,0:T(8,128)S(1)}, u32[]{:S(2)}, u32[]{:S(2)}) collective-permute-start(f32[8,256]{1,0:T(8,128)S(1)} %pad_maximum_fusion), channel_id=1, source_target_pairs={{0,1},{1,0},{2,3},{3,2},{4,5},{5,4},{6,7},{7,6},{8,9},{9,8},{10,11... | collective-permute-start | bytes 24584 | tf_op jit(solution)/shard_map/ppermute | solution.py:101
  5.6 4.7 %collective-permute-start.1 = (f32[8,256]{1,0:T(8,128)S(1)}, f32[8,256]{1,0:T(8,128)S(1)}, u32[]{:S(2)}, u32[]{:S(2)}) collective-permute-start(f32[8,256]{1,0:T(8,128)S(1)} %pad_maximum_fusion.1), channel_id=1, source_target_pairs={{0,2},{1,3},{2,0},{3,1},{4,6},{5,7},{6,4},{7,5},{8,10},{9,11},{10,... | collective-permute-start | bytes 24584 | tf_op jit(solution)/shard_map/ppermute | solution.py:101
  8.7 0.7 %copy-start = (f32[8,256]{1,0:T(8,128)S(1)}, f32[8,256]{1,0:T(8,128)}, u32[]{:S(2)}) copy-start(f32[8,256]{1,0:T(8,128)} %shard_map.64.numbers_in) | copy-start | bytes 24580
  10.4 5.2 %collective-permute-start.2 = (f32[24,256]{1,0:T(8,128)S(1)}, f32[24,256]{1,0:T(8,128)S(1)}, u32[]{:S(2)}, u32[]{:S(2)}) collective-permute-start(f32[24,256]{1,0:T(8,128)S(1)} %concatenate.11.refs_0_.payload_in), channel_id=1, source_target_pairs={{0,4},{4,8},{8,12},{12,16},{16,20},{20,24},{24,28},{28,0},{1,5},{5... | collective-permute-start | bytes 73736 | tf_op jit(solution)/shard_map/ppermute | solution.py:343
  18.1 8.8 %collective-permute-start.4 = (f32[256,256]{1,0:T(8,128)S(1)}, f32[256,256]{1,0:T(8,128)S(1)}, u32[]{:S(2)}, u32[]{:S(2)}) collective-permute-start(f32[256,256]{1,0:T(8,128)S(1)} %get-tuple-element.32), channel_id=1, source_target_pairs={{0,1},{1,2},{2,3},{3,0},{4,5},{5,6},{6,7},{7,4},{8,9},{9,10},{10,1... | collective-permute-start | bytes 786440 | tf_op jit(solution)/shard_map/ppermute | solution.py:348
